TPU v7x, 32 devices: a whole 2x2x4 slice. The times are simulated.
32 devices in a mesh: groups: 2 (over x), expert: 16 (over z, y, core).
Axes of the slice: x: 2, y: 2, z: 4, core: 2. Of those that a mesh axis runs over, the one named last changes fastest.
Arguments:
- tokens: bfloat16 [512, 2048], P(('groups', 'expert')), parts along dimension 0, may hold values from -6 to 6
- depths: int32 [512], P(('groups', 'expert')), parts along dimension 0, may hold values from 1 to 2
- routes: int32 [2, 512, 8], P(None, ('groups', 'expert')), parts along dimension 1, may hold values from 0 to 15, all different within a row; in each aligned block of 16 rows (0 to 15, 16 to 31, ..., all dimensions but the last counted through in order) at most 16 rows name the same one
- norm_gain: bfloat16 [2048], replicated, may hold values from 0.099609375 to 1.8984375
- router: bfloat16 [2048, 16], replicated, may hold values from -0.125 to 0.125
- w_gate: bfloat16 [16, 2048, 768], P('expert'), may hold values from -0.125 to 0.125
- w_up: bfloat16 [16, 2048, 768], P('expert'), may hold values from -0.125 to 0.125
- w_down: bfloat16 [16, 768, 2048], P('expert'), may hold values from -0.21875 to 0.21875
- replica_plan: int32 [16], replicated, may hold values from 0 to 15, as said below
- copy_choice: int32 [16, 16], P('expert'), may hold values from 0 to 15, as said below
Outputs:
- final_state: bfloat16 [512, 2048], P(('groups', 'expert')), parts along dimension 0
- copy_load: float32 [32, 4], P(('groups', 'expert')), parts along dimension 0
There are 2 independent parts, one for each index of `groups`. A program takes and returns all parts, laid end to end along the dimension named above; an argument that names none is the same for every part. Nothing has to cross between parts.
Inputs may be any that keep to these rules, and one draw needn't show every extreme that they name: `routes`: in each pass the 8 experts of a row differ, and no expert is named by more than 16 rows of one device (an aligned block of 16 rows); some expert is named by exactly 16 rows in some blocks. replica_plan[d] is never d. copy_choice[s, e] is a device number.
All inputs are finite; a program needn't handle non-finite values.
Results may differ from a plain program's by a relative error of at most 0.0038.
The roundings to bfloat16 on the way count: a program that leaves them out, or rounds other values in their place, can miss the bound.
Values may be sent and summed in bfloat16 or wider, within the bound.
A program may use at most 64 MiB of HBM per device.

v0:
```python
import jax
import jax.numpy as jnp
from jax import lax
from jax.sharding import PartitionSpec as P


def expert_ffn(rows_in, gate_w, up_w, down_w):
    gate_val = jnp.dot(rows_in, gate_w, preferred_element_type=jnp.float32)
    up_val = jnp.dot(rows_in, up_w, preferred_element_type=jnp.float32)
    hidden = (jax.nn.silu(gate_val) * up_val).astype(jnp.bfloat16)
    return jnp.dot(hidden, down_w, preferred_element_type=jnp.float32).astype(jnp.bfloat16)


def body(
    tokens, depths, routes, norm_gain, router, w_gate, w_up, w_down, replica_plan, copy_choice
):
    highest = lax.Precision.HIGHEST
    peer_count = lax.axis_size("expert")
    row_count, model_width = tokens.shape
    iter_count, _, top_count = routes.shape
    cap_rows = 2 * row_count * top_count // peer_count
    expert_ids = jnp.arange(peer_count, dtype=jnp.int32)
    copy_row = copy_choice[0]
    home_gate, home_up, home_down = (w_gate[0], w_up[0], w_down[0])
    onehot_all = routes[:, :, :, None] == expert_ids
    wanted_all = jnp.sum(jnp.where(onehot_all, copy_row, 0), axis=3)
    plan_at = jnp.sum(jnp.where(wanted_all[..., None] == expert_ids, replica_plan, 0), axis=3)
    valid_all = (plan_at == routes) & (wanted_all != routes)
    target_all = jnp.where(valid_all, wanted_all, routes)
    slot_all = valid_all.astype(jnp.int32)
    active_all = depths[None, :] > jnp.arange(iter_count, dtype=jnp.int32)[:, None]
    live_all = jnp.broadcast_to(active_all[:, :, None], routes.shape)
    bucket_all = target_all * 2 + slot_all
    bucket_hot = (bucket_all[..., None] == jnp.arange(2 * peer_count, dtype=jnp.int32)) & live_all[
        ..., None
    ]
    counts = jnp.sum(bucket_hot.astype(jnp.float32), axis=(1, 2)).reshape(iter_count, peer_count, 2)
    counts = jnp.transpose(counts, (1, 0, 2)).reshape(peer_count, 2 * iter_count)
    copy_load = lax.psum_scatter(counts, "expert", scatter_dimension=0, tiled=True) / float(
        row_count * top_count
    )
    slot_count = 1
    pair_rows = jnp.repeat(jnp.arange(row_count, dtype=jnp.int32), top_count)
    buffer_rows = peer_count * cap_rows * slot_count
    state = tokens
    for layer_step in range(iter_count):
        state32 = state.astype(jnp.float32)
        scale = lax.rsqrt(jnp.mean(state32 * state32, axis=1, keepdims=True) + 1e-06)
        normed = (state32 * scale * norm_gain.astype(jnp.float32)).astype(jnp.bfloat16)
        logits = jnp.dot(normed, router, preferred_element_type=jnp.float32)
        picked = jnp.sum(jnp.where(onehot_all[layer_step], logits[:, None, :], 0.0), axis=2)
        sigmas = jax.nn.sigmoid(picked)
        gates = sigmas / jnp.sum(sigmas, axis=1, keepdims=True)
        target_dev = routes[layer_step]
        live_pairs = live_all[layer_step].reshape(-1)
        bucket = (target_dev * slot_count).reshape(-1)
        bucket_flags = (
            (bucket[:, None] == jnp.arange(peer_count * slot_count, dtype=jnp.int32))
            & live_pairs[:, None]
        ).astype(jnp.int32)
        rank_table = jnp.cumsum(bucket_flags, axis=0)
        position = jnp.sum(rank_table * bucket_flags, axis=1) - 1
        index_flat = (target_dev.reshape(-1) * cap_rows + position) * slot_count
        send_index = jnp.where(live_pairs, index_flat, buffer_rows)
        outbound = (
            jnp.zeros((buffer_rows, model_width), jnp.bfloat16)
            .at[send_index]
            .set(normed[pair_rows], mode="drop")
        )
        outbound = outbound.reshape(peer_count, cap_rows, slot_count, model_width)
        received = lax.all_to_all(outbound, "expert", split_axis=0, concat_axis=0, tiled=True)
        count = received.shape[1]
        first_rows = received[:, :, 0, :].reshape(peer_count * count, model_width)
        result = expert_ffn(first_rows, home_gate, home_up, home_down).reshape(
            peer_count, count, 1, model_width
        )
        returned = lax.all_to_all(result, "expert", split_axis=0, concat_axis=0, tiled=True)
        read_index = jnp.where(live_pairs, index_flat, 0)
        pair_out = returned.reshape(buffer_rows, model_width)[read_index].reshape(
            row_count, top_count, model_width
        )
        weights = gates * live_all[layer_step].astype(jnp.float32)
        delta = jnp.einsum("rk,rkd->rd", weights, pair_out.astype(jnp.float32), precision=highest)
        state = (state32 + delta).astype(jnp.bfloat16)
    return (state, copy_load)


def solution(mesh):
    return jax.shard_map(
        body,
        mesh=mesh,
        in_specs=(
            P(("groups", "expert"), None),
            P(("groups", "expert")),
            P(None, ("groups", "expert"), None),
            P(),
            P(),
            P("expert", None, None),
            P("expert", None, None),
            P("expert", None, None),
            P(),
            P("expert", None),
        ),
        out_specs=(P(("groups", "expert"), None), P(("groups", "expert"), None)),
        check_vma=False,
    )
```

profile of v0, /device:TPU:0, one launch (start us, length us, event | category | flops | bytes accessed | tf_op | source)
XLA Modules:
  0.0 190.5 jit_solution(3896953000903324033)
XLA Ops:
  0.6 0.8 iota_compare_fusion.5
  1.7 1.0 fusion.46
  2.7 0.7 convert_element_type.51
  3.5 0.7 fusion.67
  5.0 0.9 fusion.48
  6.0 4.1 %scatter_custom_fusion = bf16[256,2048]{1,0:T(8,128)(2,1)} fusion(s32[128]{0:T(128)S(1)} %get-tuple-element.19, bf16[16,2048]{1,0:T(8,128)(2,1)S(1)} %fusion.48, s32[1024]{0:T(1024)S(1)} %pad_clamp_fusion.2, bf16[]{:T(256)} %constant.33.clone.1), kind=kCustom, calls=%fused_computation.30 | custom fusion | bytes 1048578 | tf_op jit(solution)/shard_map/scatter | solution.py:68
  10.1 32.2 %all_to_all.20 = bf16[16,16,1,2048]{3,1,2,0:T(8,128)(2,1)S(1)} all-to-all(bf16[16,16,1,2048]{3,1,2,0:T(8,128)(2,1)} %bitcast.113), channel_id=1, replica_groups=mesh['groups'=2,'expert'=16] {'expert'}, dimensions={0} | all-to-all | bytes 2097152 | tf_op jit(solution)/shard_map/all_to_all | solution.py:71
  42.3 1.0 copy-done.1
  43.4 3.8 %fusion.10 = f32[256,768]{1,0:T(8,128)} fusion(bf16[256,2048]{1,0:T(8,128)(2,1)S(1)} %bitcast.116, bf16[1,2048,768]{2,1,0:T(8,128)(2,1)} %param.15), kind=kOutput, calls=%fused_computation.16 | convolution fusion | flops 805306368 | bytes 4980736 | tf_op jit(solution)/shard_map/dot_general | solution.py:8
  47.1 5.5 %fusion.12 = bf16[256,2048]{1,0:T(8,128)(2,1)} fusion(bf16[1,768,2048]{2,1,0:T(8,128)(2,1)S(1)} %copy-done, bf16[256,2048]{1,0:T(8,128)(2,1)} %bitcast.117, bf16[1,2048,768]{2,1,0:T(8,128)(2,1)} %param.16, f32[256,768]{1,0:T(8,128)} %fusion.10), kind=kOutput, calls=%fused_computation.18 | convolution fusion | flops 1612316672 | bytes 9175040 | tf_op jit(solution)/shard_map/dot_general | solution.py:11
  52.7 5.0 %all-to-all-start.1 = ((bf16[16,16,1,2048]{3,1,2,0:T(8,128)(2,1)}), bf16[16,16,1,2048]{3,1,2,0:T(8,128)(2,1)}, u32[]{:S(2)}, u32[]{:S(2)}) async-start(bf16[16,16,1,2048]{3,1,2,0:T(8,128)(2,1)} %bitcast.115), calls=%async_computation.1 | async-start | bytes 2097152 | tf_op jit(solution)/shard_map/all_to_all | solution.py:77
  59.5 21.2 %all-to-all-done.1 = bf16[16,16,1,2048]{3,1,2,0:T(8,128)(2,1)} async-done(((bf16[16,16,1,2048]{3,1,2,0:T(8,128)(2,1)}), bf16[16,16,1,2048]{3,1,2,0:T(8,128)(2,1)}, u32[]{:S(2)}, u32[]{:S(2)}) %all-to-all-start.1) | async-done | bytes 1048608 | tf_op jit(solution)/shard_map/all_to_all | solution.py:77
  80.7 3.6 %gather_fusion = bf16[128,2048]{1,0:T(8,128)(2,1)} fusion(bf16[256,2048]{1,0:T(8,128)(2,1)} %bitcast.14, s32[1024]{0:T(1024)S(1)} %pad_clamp_fusion.1), kind=kCustom, calls=%fused_computation.1 | custom fusion | bytes 1049088 | tf_op jit(solution)/shard_map/gather | solution.py:79
  84.3 1.6 fusion.36
  86.2 4.1 %scatter_custom_fusion.1 = bf16[256,2048]{1,0:T(8,128)(2,1)} fusion(s32[128]{0:T(128)S(1)} %get-tuple-element.17, bf16[16,2048]{1,0:T(8,128)(2,1)S(1)} %fusion.52, s32[1024]{0:T(1024)S(1)} %pad_clamp_fusion.2, bf16[]{:T(256)} %constant.33.clone.1), kind=kCustom, calls=%fused_computation.28 | custom fusion | bytes 1048578 | tf_op jit(solution)/shard_map/scatter | solution.py:68
  90.3 31.7 %all_to_all.21 = bf16[16,16,1,2048]{3,1,2,0:T(8,128)(2,1)S(1)} all-to-all(bf16[16,16,1,2048]{3,1,2,0:T(8,128)(2,1)} %bitcast.112), channel_id=1, replica_groups=mesh['groups'=2,'expert'=16] {'expert'}, dimensions={0} | all-to-all | bytes 2097152 | tf_op jit(solution)/shard_map/all_to_all | solution.py:71
  122.0 1.0 copy-done.2
  123.1 3.8 %fusion.8 = f32[256,768]{1,0:T(8,128)} fusion(bf16[256,2048]{1,0:T(8,128)(2,1)S(1)} %bitcast.118, bf16[1,2048,768]{2,1,0:T(8,128)(2,1)} %param.15), kind=kOutput, calls=%fused_computation.14 | convolution fusion | flops 805306368 | bytes 4980736 | tf_op jit(solution)/shard_map/dot_general | solution.py:8
  126.8 5.5 %fusion.15 = bf16[256,2048]{1,0:T(8,128)(2,1)} fusion(bf16[1,768,2048]{2,1,0:T(8,128)(2,1)S(1)} %copy-done, bf16[256,2048]{1,0:T(8,128)(2,1)} %bitcast.119, bf16[1,2048,768]{2,1,0:T(8,128)(2,1)} %param.16, f32[256,768]{1,0:T(8,128)} %fusion.8), kind=kOutput, calls=%fused_computation.19 | convolution fusion | flops 1612316672 | bytes 9175040 | tf_op jit(solution)/shard_map/dot_general | solution.py:11
  132.4 5.0 %all-to-all-start.3 = ((bf16[16,16,1,2048]{3,1,2,0:T(8,128)(2,1)}), bf16[16,16,1,2048]{3,1,2,0:T(8,128)(2,1)}, u32[]{:S(2)}, u32[]{:S(2)}) async-start(bf16[16,16,1,2048]{3,1,2,0:T(8,128)(2,1)} %bitcast.114), calls=%async_computation.3 | async-start | bytes 2097152 | tf_op jit(solution)/shard_map/all_to_all | solution.py:77
  139.8 43.0 %all-reduce = f32[16,4]{0,1:T(4,128)S(1)} all-reduce(f32[16,4]{0,1:T(4,128)S(1)} %bitcast.123), channel_id=2, replica_groups=mesh['groups'=2,'expert'=16] {'expert'}, use_global_device_ids=true, to_apply=%region_15.16.clone | all-reduce | flops 64 | bytes 512
  182.8 0.7 dynamic-slice_multiply_fusion
  184.6 3.6 %gather_fusion.1 = bf16[128,2048]{1,0:T(8,128)(2,1)} fusion(bf16[256,2048]{1,0:T(8,128)(2,1)} %bitcast.28, s32[1024]{0:T(1024)S(1)} %pad_clamp_fusion), kind=kCustom, calls=%fused_computation.3 | custom fusion | bytes 1049088 | tf_op jit(solution)/shard_map/gather | solution.py:79
  188.2 1.6 fusion.34
  (69 shorter events, 7.1 us)
Async XLA Ops:
  0.6 46.5 %copy-start = (bf16[1,768,2048]{2,1,0:T(8,128)(2,1)S(1)}, bf16[1,768,2048]{2,1,0:T(8,128)(2,1)}, u32[]{:S(2)}) copy-start(bf16[1,768,2048]{2,1,0:T(8,128)(2,1)} %param.17) | copy-start | bytes 9437188
  42.3 1.0 copy-start.1
  47.1 10.9 %copy-start.5 = (s32[2,16,8]{1,2,0:T(8,128)S(1)}, s32[2,16,8]{1,2,0:T(8,128)}, u32[]{:S(2)}) copy-start(s32[2,16,8]{1,2,0:T(8,128)} %param.12) | copy-start | bytes 3076
  47.1 11.7 %copy-start.4 = (bf16[2048,16]{0,1:T(8,128)(2,1)S(1)}, bf16[2048,16]{0,1:T(8,128)(2,1)}, u32[]{:S(2)}) copy-start(bf16[2048,16]{0,1:T(8,128)(2,1)} %param.14) | copy-start | bytes 196612
  52.7 28.0 %all-to-all-start.1 = ((bf16[16,16,1,2048]{3,1,2,0:T(8,128)(2,1)}), bf16[16,16,1,2048]{3,1,2,0:T(8,128)(2,1)}, u32[]{:S(2)}, u32[]{:S(2)}) async-start(bf16[16,16,1,2048]{3,1,2,0:T(8,128)(2,1)} %bitcast.115), calls=%async_computation.1 | async-start | bytes 2097152 | tf_op jit(solution)/shard_map/all_to_all | solution.py:77
  57.7 28.2 %copy-start.3 = (bf16[16,2048]{1,0:T(8,128)(2,1)S(1)}, bf16[16,2048]{1,0:T(8,128)(2,1)}, u32[]{:S(2)}) copy-start(bf16[16,2048]{1,0:T(8,128)(2,1)} %param.10) | copy-start | bytes 196612
  122.0 1.0 copy-start.2
  126.8 10.6 %copy-start.6 = (s32[1,16]{1,0:T(1,128)S(1)}, s32[1,16]{1,0:T(1,128)}, u32[]{:S(2)}) copy-start(s32[1,16]{1,0:T(1,128)} %param.19) | copy-start | bytes 196
  126.8 11.3 %copy-start.7 = (s32[16]{0:T(128)S(1)}, s32[16]{0:T(128)}, u32[]{:S(2)}) copy-start(s32[16]{0:T(128)} %param.18) | copy-start | bytes 196
  126.8 12.3 %copy-start.8 = (u32[32]{0:T(128)S(1)}, u32[32]{0:T(128)}, u32[]{:S(2)}) copy-start(u32[32]{0:T(128)} %constant.49) | copy-start | bytes 388
  132.4 52.2 %all-to-all-start.3 = ((bf16[16,16,1,2048]{3,1,2,0:T(8,128)(2,1)}), bf16[16,16,1,2048]{3,1,2,0:T(8,128)(2,1)}, u32[]{:S(2)}, u32[]{:S(2)}) async-start(bf16[16,16,1,2048]{3,1,2,0:T(8,128)(2,1)} %bitcast.114), calls=%async_computation.3 | async-start | bytes 2097152 | tf_op jit(solution)/shard_map/all_to_all | solution.py:77
where the time goes:
time: 191 us; the launch traced here: 190 us
  blocking collectives  107 us (56%)
  matrix products  22.1 us (12%)
  waiting for transfers between devices  21.3 us (11%)
  local copies, waits for them, and re-layouts  20.2 us (11%)
  starting transfers between devices  10.1 us (5%)
  other arithmetic  8.94 us (5%)
    all_to_all x2, blocking collectives, body(): lax.all_to_all(outbound, 'expert', split_axis=0, concat_axis=0, tiled=True)  63.9 us
    unnamed x1, blocking collectives  43 us
    all_to_all x2, waiting for transfers between devices, body(): lax.all_to_all(result, 'expert', split_axis=0, concat_axis=0, tiled=True)  21.3 us
    dot_general x2, matrix products, expert_ffn(): jnp.dot(hidden, down_w, preferred_element_type=jnp.float32)  11.1 us
    all_to_all x2, starting transfers between devices, body(): lax.all_to_all(result, 'expert', split_axis=0, concat_axis=0, tiled=True)  10.1 us
    scatter x2, local copies, waits for them, and re-layouts, body(): outbound = jnp.zeros((buffer_rows, model_width), jnp.bfloat16).at[send_in...  8.22 us
    dot_general x2, matrix products, expert_ffn(): gate_val = jnp.dot(rows_in, gate_w, preferred_element_type=jnp.float32)  7.55 us
    gather x2, local copies, waits for them, and re-layouts, body(): returned.reshape(buffer_rows, model_width)[read_index]  7.18 us
  transfers between devices with their start and end apart: 2, of which 1 were waited for; matrix products, arithmetic and copies ran while one was open for 3% of the time, Pallas kernels for 0%

commit v1 on v0

--- a/solution.py
+++ b/solution.py
@@ -1,7 +1,315 @@
+import functools
+
 import jax
 import jax.numpy as jnp
 from jax import lax
+from jax.experimental import pallas as pl
+from jax.experimental.pallas import tpu as pltpu
 from jax.sharding import PartitionSpec as P
+
+LANES = 128
+FLAG = 32
+LOADS = 48
+CORES, CHIPS_Y, CHIPS_Z = 2, 2, 4
+FUSED_DEVICES = CORES * CHIPS_Y * CHIPS_Z
+CHUNKS = 4
+TILE = 256
+
+
+def fused_kernel(
+    tokens, depths, routes, gain, router, gate_hbm, up_hbm, down_hbm, plan, choice,
+    out, load,
+    w_gate, w_up, w_down, state, counts, rows_all, hidden, gate_col,
+    part, from_core, for_y, from_y, for_z, from_z,
+    weight_sem, gather_send, gather_recv, core_send, core_recv, y_send, y_recv, z_send, z_recv,
+):
+    me = lax.axis_index("expert")
+    core = me % CORES
+    y = (me // CORES) % CHIPS_Y
+    z = me // (CORES * CHIPS_Y)
+    other_core, other_y = 1 - core, 1 - y
+    other_z = (z + 1 - 2 * (z % 2), (z + 2) % CHIPS_Z, CHIPS_Z - 1 - z)
+
+    def device(at_z, at_y, at_core):
+        return {"expert": (at_z * CHIPS_Y + at_y) * CORES + at_core}
+
+    def slot(at_core, at_y, at_z):
+        return (at_core * CHIPS_Y + at_y) * CHIPS_Z + at_z
+
+    sibling = device(z, y, other_core)
+    across = device(z, other_y, core)
+    along = [device(at, y, core) for at in other_z]
+
+    iter_count, row_count, top_count = routes.shape
+    width = tokens.shape[1]
+    hidden_width = w_gate.shape[1]
+    all_rows = FUSED_DEVICES * row_count
+    chunk = width // CHUNKS
+    half = CHIPS_Y * CHIPS_Z
+
+    weights = [
+        pltpu.make_async_copy(src.at[0], dst, weight_sem.at[i])
+        for i, (src, dst) in enumerate(((gate_hbm, w_gate), (up_hbm, w_up), (down_hbm, w_down)))
+    ]
+    for copy in weights:
+        copy.start()
+
+    barrier = pltpu.get_barrier_semaphore()
+    for peer in (sibling, across, *along):
+        pl.semaphore_signal(barrier, inc=1, device_id=peer, device_id_type=pl.DeviceIdType.MESH)
+
+    def send(src, dst, send_sem, recv_sem, peer):
+        copy = pltpu.make_async_remote_copy(
+            src_ref=src, dst_ref=dst, send_sem=send_sem, recv_sem=recv_sem,
+            device_id=peer, device_id_type=pl.DeviceIdType.MESH,
+        )
+        copy.start()
+        return copy
+
+    def arrived(dst, send_sem, recv_sem):
+        pltpu.make_async_remote_copy(
+            src_ref=dst, dst_ref=dst, send_sem=send_sem, recv_sem=recv_sem,
+            device_id=sibling, device_id_type=pl.DeviceIdType.MESH,
+        ).wait_recv()
+
+    square = (FUSED_DEVICES, FUSED_DEVICES)
+    sub = lax.broadcasted_iota(jnp.int32, square, 0)
+    lane = lax.broadcasted_iota(jnp.int32, square, 1)
+    depth_col = jnp.sum(jnp.where(sub == lane, depths[...], 0), axis=1, keepdims=True)
+    side_lane = lax.broadcasted_iota(jnp.int32, (row_count, LANES), 1)
+
+    def route_mask(t):
+        chosen = routes[t]
+        hit = side_lane == chosen[:, 0:1]
+        for k in range(1, top_count):
+            hit = hit | (side_lane == chosen[:, k : k + 1])
+        return hit
+
+    state[...] = tokens[...].astype(jnp.float32)
+    counts[...] = jnp.zeros_like(counts)
+
+    @pl.loop(0, iter_count)
+    def one_pass(t):
+        state32 = state[...]
+        scale = lax.rsqrt(jnp.mean(state32 * state32, axis=1, keepdims=True) + 1e-06)
+        normed = (state32 * scale * gain[...].astype(jnp.float32)).astype(jnp.bfloat16)
+        active = depth_col > t
+        side = jnp.where(route_mask(t), 1.0, 0.0) + counts[...]
+        side = jnp.where((side_lane == FLAG) & active, 1.0, side)
+        mine = slot(core, y, z)
+        rows = rows_all.at[t]
+        rows[mine, :, :width] = normed
+        rows[mine, :, width:] = side.astype(jnp.bfloat16)
+
+        @pl.when(t == 0)
+        def _():
+            pl.semaphore_wait(barrier, 5)
+
+        sent = []
+
+        def share(at, peer):
+            k = len(sent)
+            sent.append(
+                send(rows.at[at], rows.at[at], gather_send.at[t, k], gather_recv.at[t, at], peer)
+            )
+
+        def landed(at):
+            arrived(rows.at[at], gather_send.at[t, 0], gather_recv.at[t, at])
+
+        share(mine, across)
+        for peer in (along[1], along[2], along[0]):
+            share(mine, peer)
+        share(mine, sibling)
+
+        @pl.when(t == 0)
+        def _():
+            copy_of = choice[...]
+            plan_col = jnp.sum(jnp.where(sub == lane, plan[...], 0), axis=1, keepdims=True)
+            plan_at = jnp.sum(jnp.where(copy_of == sub, plan_col, 0), axis=0, keepdims=True)
+            expert_row = lane[0:1]
+            valid = (plan_at == expert_row) & (copy_of != expert_row)
+            target = jnp.where(valid, copy_of, expert_row)
+            second = valid.astype(jnp.int32)
+            table = jnp.zeros((row_count, LANES), jnp.float32)
+            for step in range(iter_count):
+                live = jnp.where(route_mask(step) & (depth_col > step), 1.0, 0.0)
+                named = jnp.sum(live, axis=0, keepdims=True)[:, :FUSED_DEVICES]
+                for bit in range(2):
+                    serves = (target == sub) & (second == bit)
+                    column = jnp.sum(jnp.where(serves, named, 0.0), axis=1, keepdims=True)
+                    table = jnp.where(side_lane == LOADS + 2 * step + bit, column, table)
+            counts[...] = table
+
+        for at_z in other_z:
+            at = slot(core, y, at_z)
+            landed(at)
+            share(at, across)
+            share(at, sibling)
+        for at_z in (z, *other_z):
+            at = slot(core, other_y, at_z)
+            landed(at)
+            share(at, sibling)
+        for at_y, at_z in [(y, z)] + [(y, a) for a in other_z] + [(other_y, a) for a in (z, *other_z)]:
+            landed(slot(other_core, at_y, at_z))
+
+        @pl.when(t == 0)
+        def _():
+            weights[0].wait()
+            weights[1].wait()
+
+        def flat_rows():
+            return rows[:, :, :width].reshape(all_rows, width)
+
+        @pl.loop(0, hidden_width // TILE)
+        def _(i):
+            at = pl.ds(pl.multiple_of(i * TILE, TILE), TILE)
+            x = flat_rows()
+            gate_val = jnp.dot(x, w_gate[:, at], preferred_element_type=jnp.float32)
+            up_val = jnp.dot(x, w_up[:, at], preferred_element_type=jnp.float32)
+            silu = gate_val / (1.0 + jnp.exp(-gate_val))
+            hidden[:, at] = (silu * up_val).astype(jnp.bfloat16)
+
+        side_all = rows[:, :, width:].reshape(all_rows, LANES).astype(jnp.float32)
+        logits = jnp.dot(flat_rows(), router[...], preferred_element_type=jnp.float32)
+        sigma = side_all[:, :FUSED_DEVICES] / (1.0 + jnp.exp(-logits))
+        gates = sigma / jnp.sum(sigma, axis=1, keepdims=True)
+        all_lane = lax.broadcasted_iota(jnp.int32, (all_rows, FUSED_DEVICES), 1)
+        gate_col[...] = side_all[:, FLAG : FLAG + 1] * jnp.sum(
+            jnp.where(all_lane == me, gates, 0.0), axis=1, keepdims=True
+        )
+
+        @pl.when(t == iter_count - 1)
+        def _():
+            total = jnp.sum(rows[:, :, width:].astype(jnp.float32), axis=0)
+            row_at = lax.broadcasted_iota(jnp.int32, total.shape, 0)
+            own = jnp.sum(jnp.where(row_at == me, total, 0.0), axis=0, keepdims=True)
+            load[...] = own[:, LOADS : LOADS + 2 * iter_count] / float(row_count * top_count)
+
+        @pl.when(t == 0)
+        def _():
+            weights[2].wait()
+
+        def to_core(c):
+            span = pl.ds(other_core * half, half)
+            return send(
+                part.at[t, c, span], from_core.at[t, c], core_send.at[t, c], core_recv.at[t, c], sibling
+            )
+
+        def to_y(c):
+            arrived(from_core.at[t, c], core_send.at[t, c], core_recv.at[t, c])
+            for_y[t, c] = (
+                part[t, c, pl.ds(slot(core, other_y, 0), CHIPS_Z)].astype(jnp.float32)
+                + from_core[t, c, pl.ds(other_y * CHIPS_Z, CHIPS_Z)].astype(jnp.float32)
+            ).astype(jnp.bfloat16)
+            return send(for_y.at[t, c], from_y.at[t, c], y_send.at[t, c], y_recv.at[t, c], across)
+
+        def summed(c, at_z):
+            return (
+                part[t, c, slot(core, y, at_z)].astype(jnp.float32)
+                + from_core[t, c, y * CHIPS_Z + at_z].astype(jnp.float32)
+                + from_y[t, c, at_z].astype(jnp.float32)
+            )
+
+        def to_z(c):
+            arrived(from_y.at[t, c], y_send.at[t, c], y_recv.at[t, c])
+            copies = []
+            for i in (1, 2, 0):
+                for_z[t, c, i] = summed(c, other_z[i]).astype(jnp.bfloat16)
+                copies.append(
+                    send(
+                        for_z.at[t, c, i], from_z.at[t, c, i],
+                        z_send.at[t, c, i], z_recv.at[t, c, i], along[i],
+                    )
+                )
+            return copies
+
+        def finish(c):
+            total = summed(c, z)
+            for i in range(CHIPS_Z - 1):
+                arrived(from_z.at[t, c, i], z_send.at[t, c, i], z_recv.at[t, c, i])
+                total = total + from_z[t, c, i].astype(jnp.float32)
+            at = slice(c * chunk, (c + 1) * chunk)
+            state[:, at] = (state[:, at] + total).astype(jnp.bfloat16).astype(jnp.float32)
+
+        for c in range(CHUNKS):
+            outs = jnp.dot(
+                hidden[...], w_down[:, c * chunk : (c + 1) * chunk],
+                preferred_element_type=jnp.float32,
+            )
+            outs = outs.astype(jnp.bfloat16).astype(jnp.float32) * gate_col[...]
+            part[t, c] = outs.astype(jnp.bfloat16).reshape(FUSED_DEVICES, row_count, chunk)
+            sent.append(to_core(c))
+            if c >= 1:
+                sent.append(to_y(c - 1))
+        sent.append(to_y(CHUNKS - 1))
+        for c in range(CHUNKS):
+            sent.extend(to_z(c))
+        for c in range(CHUNKS):
+            finish(c)
+        for copy in sent:
+            copy.wait_send()
+
+    out[...] = state[...].astype(jnp.bfloat16)
+
+
+def fused_body(
+    tokens, depths, routes, norm_gain, router, w_gate, w_up, w_down, replica_plan, copy_choice
+):
+    row_count, width = tokens.shape
+    iter_count = routes.shape[0]
+    hidden_width = w_gate.shape[2]
+    all_rows = FUSED_DEVICES * row_count
+    chunk = width // CHUNKS
+    bf16, f32 = jnp.bfloat16, jnp.float32
+    dma = pltpu.SemaphoreType.DMA
+    vmem = pl.BlockSpec(memory_space=pltpu.VMEM)
+    hbm = pl.BlockSpec(memory_space=pl.ANY)
+    per_chunk = (iter_count, CHUNKS)
+    return pl.pallas_call(
+        fused_kernel,
+        out_shape=(
+            jax.ShapeDtypeStruct(tokens.shape, bf16),
+            jax.ShapeDtypeStruct((1, 2 * iter_count), f32),
+        ),
+        in_specs=[vmem] * 5 + [hbm] * 3 + [vmem] * 2,
+        out_specs=(vmem, vmem),
+        scratch_shapes=[
+            pltpu.VMEM((width, hidden_width), bf16),
+            pltpu.VMEM((width, hidden_width), bf16),
+            pltpu.VMEM((hidden_width, width), bf16),
+            pltpu.VMEM((row_count, width), f32),
+            pltpu.VMEM((row_count, LANES), f32),
+            pltpu.VMEM((iter_count, FUSED_DEVICES, row_count, width + LANES), bf16),
+            pltpu.VMEM((all_rows, hidden_width), bf16),
+            pltpu.VMEM((all_rows, 1), f32),
+            pltpu.VMEM((*per_chunk, FUSED_DEVICES, row_count, chunk), bf16),
+            pltpu.VMEM((*per_chunk, CHIPS_Y * CHIPS_Z, row_count, chunk), bf16),
+            pltpu.VMEM((*per_chunk, CHIPS_Z, row_count, chunk), bf16),
+            pltpu.VMEM((*per_chunk, CHIPS_Z, row_count, chunk), bf16),
+            pltpu.VMEM((*per_chunk, CHIPS_Z - 1, row_count, chunk), bf16),
+            pltpu.VMEM((*per_chunk, CHIPS_Z - 1, row_count, chunk), bf16),
+            dma((3,)),
+            dma((iter_count, FUSED_DEVICES)),
+            dma((iter_count, FUSED_DEVICES)),
+            dma(per_chunk),
+            dma(per_chunk),
+            dma(per_chunk),
+            dma(per_chunk),
+            dma((*per_chunk, CHIPS_Z - 1)),
+            dma((*per_chunk, CHIPS_Z - 1)),
+        ],
+        compiler_params=pltpu.CompilerParams(
+            collective_id=0, has_side_effects=True, vmem_limit_bytes=48 * 1024 * 1024
+        ),
+        cost_estimate=pl.CostEstimate(
+            flops=6 * iter_count * all_rows * width * hidden_width,
+            bytes_accessed=6 * width * hidden_width,
+            transcendentals=iter_count * all_rows * hidden_width,
+        ),
+    )(
+        tokens, depths.reshape(1, -1), routes, norm_gain.reshape(1, -1), router,
+        w_gate, w_up, w_down, replica_plan.reshape(1, -1), copy_choice,
+    )
 
 
 def expert_ffn(rows_in, gate_w, up_w, down_w):
@@ -11,7 +319,7 @@
     return jnp.dot(hidden, down_w, preferred_element_type=jnp.float32).astype(jnp.bfloat16)
 
 
-def body(
+def dispatch_body(
     tokens, depths, routes, norm_gain, router, w_gate, w_up, w_down, replica_plan, copy_choice
 ):
     highest = lax.Precision.HIGHEST
@@ -86,6 +394,7 @@
 
 
 def solution(mesh):
+    body = fused_body if mesh.shape["expert"] == FUSED_DEVICES else dispatch_body
     return jax.shard_map(
         body,
         mesh=mesh,

time: 191 us -> 69.7 us (0.36)
  blocking collectives: 107 us -> 0 us
  Pallas kernels: 0 us -> 60.2 us
  matrix products: 22.1 us -> 0 us
  waiting for transfers between devices: 21.3 us -> 0 us
  local copies, waits for them, and re-layouts: 20.2 us -> 8.41 us
  starting transfers between devices: 10.1 us -> 0 us
  other arithmetic: 8.94 us -> 0 us
    all_to_all x2 -> x0, blocking collectives: 63.9 us -> none  [body(): lax.all_to_all(outbound, 'expert', split_axis=0, concat_axis=0, tiled=True)]
    pallas_call x0 -> x1, Pallas kernels: none -> 60.2 us  [fused_body(): pl.pallas_call(fused_kernel, out_shape=(jax.ShapeDtypeStruct(tokens.shape...]
    unnamed x1 -> x0, blocking collectives: 43 us -> none
    dot_general x8 -> x0, matrix products: 22.1 us -> none  [the longest x2 11.1 us: expert_ffn(): jnp.dot(hidden, down_w, preferred_element_type=jnp.float32)]
    all_to_all x2 -> x0, waiting for transfers between devices: 21.3 us -> none  [body(): lax.all_to_all(result, 'expert', split_axis=0, concat_axis=0, tiled=True)]
    all_to_all x2 -> x0, starting transfers between devices: 10.1 us -> none  [body(): lax.all_to_all(result, 'expert', split_axis=0, concat_axis=0, tiled=True)]
    scatter x2 -> x0, local copies, waits for them, and re-layouts: 8.22 us -> none  [body(): outbound = jnp.zeros((buffer_rows, model_width), jnp.bfloat16).at[send_in...]
    gather x2 -> x0, local copies, waits for them, and re-layouts: 7.18 us -> none  [body(): returned.reshape(buffer_rows, model_width)[read_index]]
  transfers between devices with their start and end apart: 2 -> 0, of which waited for: 1 -> 0; matrix products, arithmetic and copies ran while one was open for 3% -> 0% of each run, Pallas kernels for 0% -> 0%
where the time goes in v1:
time: 69.7 us; the launch traced here: 69.3 us
  Pallas kernels  60.2 us (86%)
  local copies, waits for them, and re-layouts  8.41 us (12%)
    pallas_call x1, Pallas kernels, fused_body(): pl.pallas_call(fused_kernel, out_shape=(jax.ShapeDtypeStruct(tokens.shape...  60.2 us
    unnamed x14, local copies, waits for them, and re-layouts  7.71 us

profile of v1, /device:TPU:0, one launch (start us, length us, event | category | flops | bytes accessed | tf_op | source)
XLA Modules:
  0.0 69.3 jit_solution(7252371976280990142)
XLA Ops:
  0.6 0.7 %reshape.14.gain = bf16[1,2048]{1,0:T(2,128)(2,1)S(1)} reshape(bf16[2048]{0:T(1024)(128)(2,1)} %param.13) | data formatting | bytes 8192 | tf_op jit(solution)/shard_map/reshape | solution.py:310
  1.3 0.8 %copy.12.routes = s32[2,16,8]{2,1,0:T(8,128)S(1)} copy(s32[2,16,8]{1,2,0:T(8,128)} %param.12) | data formatting | bytes 2048 | tf_op args[2]
  2.1 1.1 %copy.13.router = bf16[2048,16]{1,0:T(8,128)(2,1)S(1)} copy(bf16[2048,16]{0,1:T(8,128)(2,1)} %param.14) | data formatting | bytes 131072 | tf_op args[4]
  3.2 0.0 copy-start
  3.2 1.9 %copy-done = bf16[1,2048,768]{2,1,0:T(8,128)(2,1)S(1)} copy-done((bf16[1,2048,768]{2,1,0:T(8,128)(2,1)S(1)}, bf16[1,2048,768]{2,1,0:T(8,128)(2,1)}, u32[]{:S(2)}) %copy-start) | copy-done | bytes 3145752
  5.1 0.0 copy-start.1
  5.1 0.8 %copy-done.1 = bf16[16,2048]{1,0:T(8,128)(2,1)S(1)} copy-done((bf16[16,2048]{1,0:T(8,128)(2,1)S(1)}, bf16[16,2048]{1,0:T(8,128)(2,1)}, u32[]{:S(2)}) %copy-start.1) | copy-done | bytes 65560
  5.9 0.0 copy-start.2
  5.9 0.7 copy-done.2
  6.6 0.0 copy-start.3
  6.6 0.7 copy-done.3
  7.3 0.0 copy-start.4
  7.3 0.7 copy-done.4
  7.9 60.2 %shard_map.113 = (bf16[16,2048]{1,0:T(8,128)(2,1)S(1)}, f32[1,4]{1,0:T(1,128)S(1)}) custom-call(bf16[16,2048]{1,0:T(8,128)(2,1)S(1)} %copy-done.1, s32[1,16]{1,0:T(1,128)S(1)} %bitcast.2, s32[2,16,8]{2,1,0:T(8,128)S(1)} %copy.12.routes, bf16[1,2048]{1,0:T(2,128)(2,1)S(1)} %reshape.14.gain, bf16[2048,16]{1,0:T(8,128)(2,1)S(1)} %copy.13.router, ...), custom_call_target="tpu_custom_call" | custom-call | flops 4831838208 | bytes 9437184 | tf_op jit(solution)/shard_map/pallas_call | solution.py:268
  68.2 0.6 copy.16
  68.8 0.5 copy.17
Async XLA Ops:
  3.2 1.9 %copy-start = (bf16[1,2048,768]{2,1,0:T(8,128)(2,1)S(1)}, bf16[1,2048,768]{2,1,0:T(8,128)(2,1)}, u32[]{:S(2)}) copy-start(bf16[1,2048,768]{2,1,0:T(8,128)(2,1)} %gate_hbm.1) | copy-start | bytes 9437188
  5.1 0.8 %copy-start.1 = (bf16[16,2048]{1,0:T(8,128)(2,1)S(1)}, bf16[16,2048]{1,0:T(8,128)(2,1)}, u32[]{:S(2)}) copy-start(bf16[16,2048]{1,0:T(8,128)(2,1)} %tokens.1) | copy-start | bytes 196612
  5.9 0.7 copy-start.2
  6.6 0.7 copy-start.3
  7.3 0.7 copy-start.4

commit v2 on v1

--- a/solution.py
+++ b/solution.py
@@ -17,11 +17,13 @@
 
 
 def fused_kernel(
-    tokens, depths, routes, gain, router, gate_hbm, up_hbm, down_hbm, plan, choice,
+    tokens_hbm, depths_hbm, routes_hbm, gain_hbm, plan_hbm, choice_hbm, router_hbm,
+    gate_hbm, up_hbm, down_hbm,
     out, load,
-    w_gate, w_up, w_down, state, counts, rows_all, hidden, gate_col,
+    tokens, depths, routes, gain, plan, choice, router, w_gate, w_up, w_down,
+    state, sides, rows_all, hidden, gate_col,
     part, from_core, for_y, from_y, for_z, from_z,
-    weight_sem, gather_send, gather_recv, core_send, core_recv, y_send, y_recv, z_send, z_recv,
+    small_sem, weight_sem, gather_send, gather_recv, core_send, core_recv, y_send, y_recv, z_send, z_recv,
 ):
     me = lax.axis_index("expert")
     core = me % CORES
@@ -33,20 +35,28 @@
     def device(at_z, at_y, at_core):
         return {"expert": (at_z * CHIPS_Y + at_y) * CORES + at_core}
 
-    def slot(at_core, at_y, at_z):
-        return (at_core * CHIPS_Y + at_y) * CHIPS_Z + at_z
-
     sibling = device(z, y, other_core)
     across = device(z, other_y, core)
     along = [device(at, y, core) for at in other_z]
 
-    iter_count, row_count, top_count = routes.shape
+    iter_count, top_count, row_count = routes.shape
     width = tokens.shape[1]
     hidden_width = w_gate.shape[1]
     all_rows = FUSED_DEVICES * row_count
     chunk = width // CHUNKS
     half = CHIPS_Y * CHIPS_Z
 
+    small = [
+        pltpu.make_async_copy(src, dst, small_sem.at[i])
+        for i, (src, dst) in enumerate(
+            (
+                (tokens_hbm, tokens), (depths_hbm, depths), (routes_hbm, routes), (gain_hbm, gain),
+                (plan_hbm, plan), (choice_hbm, choice), (router_hbm, router),
+            )
+        )
+    ]
+    for copy in small:
+        copy.start()
     weights = [
         pltpu.make_async_copy(src.at[0], dst, weight_sem.at[i])
         for i, (src, dst) in enumerate(((gate_hbm, w_gate), (up_hbm, w_up), (down_hbm, w_down)))
@@ -72,111 +82,144 @@
             device_id=sibling, device_id_type=pl.DeviceIdType.MESH,
         ).wait_recv()
 
+    for copy in small:
+        copy.wait()
     square = (FUSED_DEVICES, FUSED_DEVICES)
     sub = lax.broadcasted_iota(jnp.int32, square, 0)
     lane = lax.broadcasted_iota(jnp.int32, square, 1)
+    side_lane = lax.broadcasted_iota(jnp.int32, (row_count, LANES), 1)
+    side_sub = lax.broadcasted_iota(jnp.int32, (row_count, LANES), 0)
+    diagonal = jnp.where(side_lane == side_sub, 1.0, 0.0).astype(jnp.bfloat16)
     depth_col = jnp.sum(jnp.where(sub == lane, depths[...], 0), axis=1, keepdims=True)
-    side_lane = lax.broadcasted_iota(jnp.int32, (row_count, LANES), 1)
-
-    def route_mask(t):
-        chosen = routes[t]
-        hit = side_lane == chosen[:, 0:1]
+    state[...] = tokens[...].astype(jnp.float32)
+
+    masks = []
+    for step in range(iter_count):
+        chosen = routes[step]
+        hit = sub == chosen[0:1]
         for k in range(1, top_count):
-            hit = hit | (side_lane == chosen[:, k : k + 1])
-        return hit
-
-    state[...] = tokens[...].astype(jnp.float32)
-    counts[...] = jnp.zeros_like(counts)
+            hit = hit | (sub == chosen[k : k + 1])
+        masks.append(
+            lax.dot_general(
+                jnp.where(hit, 1.0, 0.0).astype(jnp.bfloat16), diagonal,
+                (((0,), (0,)), ((), ())), preferred_element_type=jnp.float32,
+            )
+        )
+        active = depth_col > step
+        sides[step] = jnp.where((side_lane == FLAG) & active, 1.0, masks[step])
+
+    copy_of = choice[...]
+    plan_col = jnp.sum(jnp.where(sub == lane, plan[...], 0), axis=1, keepdims=True)
+    plan_at = jnp.sum(jnp.where(copy_of == sub, plan_col, 0), axis=0, keepdims=True)
+    expert_row = lane[0:1]
+    valid = (plan_at == expert_row) & (copy_of != expert_row)
+    target = jnp.where(valid, copy_of, expert_row)
+    second = valid.astype(jnp.int32)
+    table = sides[iter_count - 1]
+    for step in range(iter_count):
+        live = jnp.where(depth_col > step, masks[step], 0.0)
+        named = jnp.sum(live, axis=0, keepdims=True)[:, :FUSED_DEVICES]
+        for bit in range(2):
+            serves = (target == sub) & (second == bit)
+            column = jnp.sum(jnp.where(serves, named, 0.0), axis=1, keepdims=True)
+            table = jnp.where(side_lane == LOADS + 2 * step + bit, column, table)
+    sides[iter_count - 1] = table
 
     @pl.loop(0, iter_count)
     def one_pass(t):
         state32 = state[...]
         scale = lax.rsqrt(jnp.mean(state32 * state32, axis=1, keepdims=True) + 1e-06)
-        normed = (state32 * scale * gain[...].astype(jnp.float32)).astype(jnp.bfloat16)
-        active = depth_col > t
-        side = jnp.where(route_mask(t), 1.0, 0.0) + counts[...]
-        side = jnp.where((side_lane == FLAG) & active, 1.0, side)
-        mine = slot(core, y, z)
+        normed = (state32 * scale * gain[...].reshape(1, width).astype(jnp.float32)).astype(jnp.bfloat16)
         rows = rows_all.at[t]
-        rows[mine, :, :width] = normed
-        rows[mine, :, width:] = side.astype(jnp.bfloat16)
+        rows[z, :, :width] = normed
+        rows[z, :, width:] = sides[t].astype(jnp.bfloat16)
 
         @pl.when(t == 0)
         def _():
             pl.semaphore_wait(barrier, 5)
 
-        sent = []
-
-        def share(at, peer):
-            k = len(sent)
-            sent.append(
-                send(rows.at[at], rows.at[at], gather_send.at[t, k], gather_recv.at[t, at], peer)
+        def share(src, dst, kind, peer):
+            return send(
+                rows.at[src], rows.at[dst], gather_send.at[t, kind, src], gather_recv.at[t, dst], peer
             )
 
         def landed(at):
-            arrived(rows.at[at], gather_send.at[t, 0], gather_recv.at[t, at])
-
-        share(mine, across)
-        for peer in (along[1], along[2], along[0]):
-            share(mine, peer)
-        share(mine, sibling)
-
-        @pl.when(t == 0)
-        def _():
-            copy_of = choice[...]
-            plan_col = jnp.sum(jnp.where(sub == lane, plan[...], 0), axis=1, keepdims=True)
-            plan_at = jnp.sum(jnp.where(copy_of == sub, plan_col, 0), axis=0, keepdims=True)
-            expert_row = lane[0:1]
-            valid = (plan_at == expert_row) & (copy_of != expert_row)
-            target = jnp.where(valid, copy_of, expert_row)
-            second = valid.astype(jnp.int32)
-            table = jnp.zeros((row_count, LANES), jnp.float32)
-            for step in range(iter_count):
-                live = jnp.where(route_mask(step) & (depth_col > step), 1.0, 0.0)
-                named = jnp.sum(live, axis=0, keepdims=True)[:, :FUSED_DEVICES]
-                for bit in range(2):
-                    serves = (target == sub) & (second == bit)
-                    column = jnp.sum(jnp.where(serves, named, 0.0), axis=1, keepdims=True)
-                    table = jnp.where(side_lane == LOADS + 2 * step + bit, column, table)
-            counts[...] = table
-
-        for at_z in other_z:
-            at = slot(core, y, at_z)
-            landed(at)
-            share(at, across)
-            share(at, sibling)
-        for at_z in (z, *other_z):
-            at = slot(core, other_y, at_z)
-            landed(at)
-            share(at, sibling)
-        for at_y, at_z in [(y, z)] + [(y, a) for a in other_z] + [(other_y, a) for a in (z, *other_z)]:
-            landed(slot(other_core, at_y, at_z))
+            arrived(rows.at[at], gather_send.at[t, 0, 0], gather_recv.at[t, at])
+
+        def to_next(at_z, up):
+            @pl.when((z < CHIPS_Z - 1) if up else (z > 0))
+            def _():
+                share(at_z, at_z, 0 if up else 1, device(z + 1 if up else z - 1, y, core))
+
+        to_next(z, True)
+        to_next(z, False)
+        share(z, CHIPS_Z + z, 2, across)
+        share(z, half + z, 3, sibling)
+        for step in range(1, CHIPS_Z):
+            for up in (True, False):
+                at_z = z - step if up else z + step
+
+                @pl.when((at_z >= 0) if up else (at_z < CHIPS_Z))
+                def _(at_z=at_z, up=up):
+                    landed(at_z)
+                    to_next(at_z, up)
+                    share(at_z, CHIPS_Z + at_z, 2, across)
+                    share(at_z, half + at_z, 3, sibling)
 
         @pl.when(t == 0)
         def _():
             weights[0].wait()
             weights[1].wait()
 
-        def flat_rows():
-            return rows[:, :, :width].reshape(all_rows, width)
-
-        @pl.loop(0, hidden_width // TILE)
-        def _(i):
-            at = pl.ds(pl.multiple_of(i * TILE, TILE), TILE)
-            x = flat_rows()
-            gate_val = jnp.dot(x, w_gate[:, at], preferred_element_type=jnp.float32)
-            up_val = jnp.dot(x, w_up[:, at], preferred_element_type=jnp.float32)
-            silu = gate_val / (1.0 + jnp.exp(-gate_val))
-            hidden[:, at] = (silu * up_val).astype(jnp.bfloat16)
-
-        side_all = rows[:, :, width:].reshape(all_rows, LANES).astype(jnp.float32)
-        logits = jnp.dot(flat_rows(), router[...], preferred_element_type=jnp.float32)
-        sigma = side_all[:, :FUSED_DEVICES] / (1.0 + jnp.exp(-logits))
-        gates = sigma / jnp.sum(sigma, axis=1, keepdims=True)
-        all_lane = lax.broadcasted_iota(jnp.int32, (all_rows, FUSED_DEVICES), 1)
-        gate_col[...] = side_all[:, FLAG : FLAG + 1] * jnp.sum(
-            jnp.where(all_lane == me, gates, 0.0), axis=1, keepdims=True
-        )
+        def half_rows(dy, lanes):
+            pieces = [
+                rows[pl.ds(dc * half + dy * CHIPS_Z, CHIPS_Z), :, lanes] for dc in range(CORES)
+            ]
+            return jnp.concatenate(pieces, axis=0).reshape(all_rows // 2, -1)
+
+        def gate_up(dy):
+            span = slice(dy * all_rows // 2, (dy + 1) * all_rows // 2)
+
+            @pl.loop(0, hidden_width // TILE)
+            def _(i):
+                at = pl.ds(pl.multiple_of(i * TILE, TILE), TILE)
+                x = half_rows(dy, slice(0, width))
+                gate_val = jnp.dot(x, w_gate[:, at], preferred_element_type=jnp.float32)
+                up_val = jnp.dot(x, w_up[:, at], preferred_element_type=jnp.float32)
+                silu = gate_val / (1.0 + jnp.exp(-gate_val))
+                hidden[span, at] = (silu * up_val).astype(jnp.bfloat16)
+
+            side = half_rows(dy, slice(width, width + LANES)).astype(jnp.float32)
+            logits = lax.dot_general(
+                half_rows(dy, slice(0, width)), router[...],
+                (((1,), (1,)), ((), ())), preferred_element_type=jnp.float32,
+            )
+            sigma = side[:, :FUSED_DEVICES] / (1.0 + jnp.exp(-logits))
+            gates = sigma / jnp.sum(sigma, axis=1, keepdims=True)
+            gate_lane = lax.broadcasted_iota(jnp.int32, gates.shape, 1)
+            gate_col[span] = side[:, FLAG : FLAG + 1] * jnp.sum(
+                jnp.where(gate_lane == me, gates, 0.0), axis=1, keepdims=True
+            )
+
+        for i in range(CHIPS_Z):
+            landed(half + i)
+        for step in range(CHIPS_Z):
+            if step == 0:
+                landed(CHIPS_Z + z)
+                share(CHIPS_Z + z, half + CHIPS_Z + z, 3, sibling)
+                continue
+            for at_z, there in ((z - step, z - step >= 0), (z + step, z + step < CHIPS_Z)):
+
+                @pl.when(there)
+                def _(at_z=at_z):
+                    landed(CHIPS_Z + at_z)
+                    share(CHIPS_Z + at_z, half + CHIPS_Z + at_z, 3, sibling)
+
+            if step == 1:
+                gate_up(0)
+        for i in range(CHIPS_Z):
+            landed(half + CHIPS_Z + i)
+        gate_up(1)
 
         @pl.when(t == iter_count - 1)
         def _():
@@ -190,23 +233,22 @@
             weights[2].wait()
 
         def to_core(c):
-            span = pl.ds(other_core * half, half)
             return send(
-                part.at[t, c, span], from_core.at[t, c], core_send.at[t, c], core_recv.at[t, c], sibling
+                part.at[t, c, pl.ds(half, half)], from_core.at[t, c], core_send.at[t, c], core_recv.at[t, c], sibling
             )
 
         def to_y(c):
             arrived(from_core.at[t, c], core_send.at[t, c], core_recv.at[t, c])
             for_y[t, c] = (
-                part[t, c, pl.ds(slot(core, other_y, 0), CHIPS_Z)].astype(jnp.float32)
-                + from_core[t, c, pl.ds(other_y * CHIPS_Z, CHIPS_Z)].astype(jnp.float32)
+                part[t, c, pl.ds(CHIPS_Z, CHIPS_Z)].astype(jnp.float32)
+                + from_core[t, c, pl.ds(CHIPS_Z, CHIPS_Z)].astype(jnp.float32)
             ).astype(jnp.bfloat16)
             return send(for_y.at[t, c], from_y.at[t, c], y_send.at[t, c], y_recv.at[t, c], across)
 
         def summed(c, at_z):
             return (
-                part[t, c, slot(core, y, at_z)].astype(jnp.float32)
-                + from_core[t, c, y * CHIPS_Z + at_z].astype(jnp.float32)
+                part[t, c, at_z].astype(jnp.float32)
+                + from_core[t, c, at_z].astype(jnp.float32)
                 + from_y[t, c, at_z].astype(jnp.float32)
             )
 
@@ -231,23 +273,43 @@
             at = slice(c * chunk, (c + 1) * chunk)
             state[:, at] = (state[:, at] + total).astype(jnp.bfloat16).astype(jnp.float32)
 
+        sent = []
         for c in range(CHUNKS):
             outs = jnp.dot(
                 hidden[...], w_down[:, c * chunk : (c + 1) * chunk],
                 preferred_element_type=jnp.float32,
             )
             outs = outs.astype(jnp.bfloat16).astype(jnp.float32) * gate_col[...]
-            part[t, c] = outs.astype(jnp.bfloat16).reshape(FUSED_DEVICES, row_count, chunk)
+            outs = outs.astype(jnp.bfloat16).reshape(FUSED_DEVICES, row_count, chunk)
+            for dy in range(CHIPS_Y):
+                for dc in range(CORES):
+                    first = (dy * CORES + dc) * CHIPS_Z
+                    part[t, c, pl.ds(dc * half + dy * CHIPS_Z, CHIPS_Z)] = outs[first : first + CHIPS_Z]
             sent.append(to_core(c))
-            if c >= 1:
-                sent.append(to_y(c - 1))
-        sent.append(to_y(CHUNKS - 1))
+            if c >= 2:
+                sent.append(to_y(c - 2))
+        for c in range(CHUNKS - 2, CHUNKS):
+            sent.append(to_y(c))
         for c in range(CHUNKS):
             sent.extend(to_z(c))
         for c in range(CHUNKS):
             finish(c)
         for copy in sent:
             copy.wait_send()
+
+        def gone(src, kind):
+            pltpu.make_async_remote_copy(
+                src_ref=rows.at[src], dst_ref=rows.at[src],
+                send_sem=gather_send.at[t, kind, src], recv_sem=gather_recv.at[t, src],
+                device_id=sibling, device_id_type=pl.DeviceIdType.MESH,
+            ).wait_send()
+
+        for at_z in range(CHIPS_Z):
+            pl.when((at_z <= z) & (z < CHIPS_Z - 1))(functools.partial(gone, at_z, 0))
+            pl.when((at_z >= z) & (z > 0))(functools.partial(gone, at_z, 1))
+            gone(at_z, 2)
+            gone(at_z, 3)
+            gone(CHIPS_Z + at_z, 3)
 
     out[...] = state[...].astype(jnp.bfloat16)
 
@@ -263,22 +325,27 @@
     bf16, f32 = jnp.bfloat16, jnp.float32
     dma = pltpu.SemaphoreType.DMA
     vmem = pl.BlockSpec(memory_space=pltpu.VMEM)
-    hbm = pl.BlockSpec(memory_space=pl.ANY)
+    hbm = pl.BlockSpec(memory_space=pltpu.HBM)
     per_chunk = (iter_count, CHUNKS)
+    small = (
+        tokens, depths.reshape(1, -1), jnp.transpose(routes, (0, 2, 1)), norm_gain,
+        replica_plan.reshape(1, -1), copy_choice, jnp.transpose(router),
+    )
     return pl.pallas_call(
         fused_kernel,
         out_shape=(
             jax.ShapeDtypeStruct(tokens.shape, bf16),
             jax.ShapeDtypeStruct((1, 2 * iter_count), f32),
         ),
-        in_specs=[vmem] * 5 + [hbm] * 3 + [vmem] * 2,
+        in_specs=[hbm] * 10,
         out_specs=(vmem, vmem),
-        scratch_shapes=[
+        scratch_shapes=[pltpu.VMEM(array.shape, array.dtype) for array in small]
+        + [
             pltpu.VMEM((width, hidden_width), bf16),
             pltpu.VMEM((width, hidden_width), bf16),
             pltpu.VMEM((hidden_width, width), bf16),
             pltpu.VMEM((row_count, width), f32),
-            pltpu.VMEM((row_count, LANES), f32),
+            pltpu.VMEM((iter_count, row_count, LANES), f32),
             pltpu.VMEM((iter_count, FUSED_DEVICES, row_count, width + LANES), bf16),
             pltpu.VMEM((all_rows, hidden_width), bf16),
             pltpu.VMEM((all_rows, 1), f32),
@@ -288,8 +355,9 @@
             pltpu.VMEM((*per_chunk, CHIPS_Z, row_count, chunk), bf16),
             pltpu.VMEM((*per_chunk, CHIPS_Z - 1, row_count, chunk), bf16),
             pltpu.VMEM((*per_chunk, CHIPS_Z - 1, row_count, chunk), bf16),
+            dma((len(small),)),
             dma((3,)),
-            dma((iter_count, FUSED_DEVICES)),
+            dma((iter_count, 4, FUSED_DEVICES)),
             dma((iter_count, FUSED_DEVICES)),
             dma(per_chunk),
             dma(per_chunk),
@@ -299,7 +367,7 @@
             dma((*per_chunk, CHIPS_Z - 1)),
         ],
         compiler_params=pltpu.CompilerParams(
-            collective_id=0, has_side_effects=True, vmem_limit_bytes=48 * 1024 * 1024
+            collective_id=0, has_side_effects=True, vmem_limit_bytes=56 * 1024 * 1024
         ),
         cost_estimate=pl.CostEstimate(
             flops=6 * iter_count * all_rows * width * hidden_width,
@@ -307,8 +375,7 @@
             transcendentals=iter_count * all_rows * hidden_width,
         ),
     )(
-        tokens, depths.reshape(1, -1), routes, norm_gain.reshape(1, -1), router,
-        w_gate, w_up, w_down, replica_plan.reshape(1, -1), copy_choice,
+        *small, w_gate, w_up, w_down,
     )
 
 

time: 69.7 us -> 70.4 us (1.010)
  Pallas kernels: 60.2 us -> 67 us
  local copies, waits for them, and re-layouts: 8.41 us -> 2.59 us
    pallas_call x1, Pallas kernels: 60.2 us -> 67 us  [fused_body(): pl.pallas_call(fused_kernel, out_shape=(jax.ShapeDtypeStruct(tokens.shape...]
    unnamed x14 -> x2, local copies, waits for them, and re-layouts: 7.71 us -> 2.59 us
where the time goes in v2:
time: 70.4 us; the launch traced here: 70.2 us
  Pallas kernels  67 us (95%)
  local copies, waits for them, and re-layouts  2.59 us (4%)
    pallas_call x1, Pallas kernels, fused_body(): pl.pallas_call(fused_kernel, out_shape=(jax.ShapeDtypeStruct(tokens.shape...  67 us
    unnamed x2, local copies, waits for them, and re-layouts  2.59 us

profile of v2, /device:TPU:0, one launch (start us, length us, event | category | flops | bytes accessed | tf_op | source)
XLA Modules:
  0.0 70.2 jit_solution(9451441398355154686)
XLA Ops:
  0.6 67.0 %shard_map.113 = (bf16[16,2048]{1,0:T(8,128)(2,1)}, f32[1,4]{1,0:T(1,128)}) custom-call(bf16[16,2048]{1,0:T(8,128)(2,1)} %tokens_hbm.1, s32[1,16]{1,0:T(1,128)} %bitcast.6, s32[2,8,16]{2,1,0:T(8,128)} %bitcast.5, bf16[2048]{0:T(1024)(128)(2,1)} %gain_hbm.1, s32[1,16]{1,0:T(1,128)} %bitcast.7, s32[1,16]{1,0:T(1,128)} %choice_hbm.1, bf16[16,2048]{1,0:T(8,128)(2,1)} %bitcast.4, ...), custom_call_target="tpu_custom_call" | custom-call | flops 4831838208 | bytes 9437184 | tf_op jit(solution)/shard_map/pallas_call | solution.py:334
  67.7 1.5 %copy.14 = bf16[16,2048]{1,0:T(8,128)(2,1)} copy(bf16[16,2048]{1,0:T(8,128)(2,1)} %get-tuple-element.4) | data formatting | bytes 131072
  69.1 1.1 %copy.15 = f32[1,4]{1,0:T(1,128)} copy(f32[1,4]{1,0:T(1,128)} %get-tuple-element.5) | data formatting | bytes 32

commit v3 on v2

--- a/solution.py
+++ b/solution.py
@@ -21,7 +21,7 @@
     gate_hbm, up_hbm, down_hbm,
     out, load,
     tokens, depths, routes, gain, plan, choice, router, w_gate, w_up, w_down,
-    state, sides, rows_all, hidden, gate_col,
+    state, sides, masks, rows_first, rows_second, partial, hidden, gate_col,
     part, from_core, for_y, from_y, for_z, from_z,
     small_sem, weight_sem, gather_send, gather_recv, core_send, core_recv, y_send, y_recv, z_send, z_recv,
 ):
@@ -93,137 +93,157 @@
     depth_col = jnp.sum(jnp.where(sub == lane, depths[...], 0), axis=1, keepdims=True)
     state[...] = tokens[...].astype(jnp.float32)
 
-    masks = []
     for step in range(iter_count):
         chosen = routes[step]
         hit = sub == chosen[0:1]
         for k in range(1, top_count):
             hit = hit | (sub == chosen[k : k + 1])
-        masks.append(
-            lax.dot_general(
-                jnp.where(hit, 1.0, 0.0).astype(jnp.bfloat16), diagonal,
-                (((0,), (0,)), ((), ())), preferred_element_type=jnp.float32,
-            )
+        masks[step] = lax.dot_general(
+            jnp.where(hit, 1.0, 0.0).astype(jnp.bfloat16), diagonal,
+            (((0,), (0,)), ((), ())), preferred_element_type=jnp.float32,
         )
         active = depth_col > step
         sides[step] = jnp.where((side_lane == FLAG) & active, 1.0, masks[step])
 
-    copy_of = choice[...]
-    plan_col = jnp.sum(jnp.where(sub == lane, plan[...], 0), axis=1, keepdims=True)
-    plan_at = jnp.sum(jnp.where(copy_of == sub, plan_col, 0), axis=0, keepdims=True)
-    expert_row = lane[0:1]
-    valid = (plan_at == expert_row) & (copy_of != expert_row)
-    target = jnp.where(valid, copy_of, expert_row)
-    second = valid.astype(jnp.int32)
-    table = sides[iter_count - 1]
-    for step in range(iter_count):
-        live = jnp.where(depth_col > step, masks[step], 0.0)
-        named = jnp.sum(live, axis=0, keepdims=True)[:, :FUSED_DEVICES]
-        for bit in range(2):
-            serves = (target == sub) & (second == bit)
-            column = jnp.sum(jnp.where(serves, named, 0.0), axis=1, keepdims=True)
-            table = jnp.where(side_lane == LOADS + 2 * step + bit, column, table)
-    sides[iter_count - 1] = table
+    def count_pairs():
+        copy_of = choice[...]
+        plan_col = jnp.sum(jnp.where(sub == lane, plan[...], 0), axis=1, keepdims=True)
+        plan_at = jnp.sum(jnp.where(copy_of == sub, plan_col, 0), axis=0, keepdims=True)
+        expert_row = lane[0:1]
+        valid = (plan_at == expert_row) & (copy_of != expert_row)
+        target = jnp.where(valid, copy_of, expert_row)
+        second = valid.astype(jnp.int32)
+        table = sides[iter_count - 1]
+        for step in range(iter_count):
+            live = jnp.where(depth_col > step, masks[step], 0.0)
+            named = jnp.sum(live, axis=0, keepdims=True)[:, :FUSED_DEVICES]
+            for bit in range(2):
+                serves = (target == sub) & (second == bit)
+                column = jnp.sum(jnp.where(serves, named, 0.0), axis=1, keepdims=True)
+                table = jnp.where(side_lane == LOADS + 2 * step + bit, column, table)
+        sides[iter_count - 1] = table
 
     @pl.loop(0, iter_count)
     def one_pass(t):
         state32 = state[...]
         scale = lax.rsqrt(jnp.mean(state32 * state32, axis=1, keepdims=True) + 1e-06)
         normed = (state32 * scale * gain[...].reshape(1, width).astype(jnp.float32)).astype(jnp.bfloat16)
-        rows = rows_all.at[t]
-        rows[z, :, :width] = normed
-        rows[z, :, width:] = sides[t].astype(jnp.bfloat16)
+        pieces = (rows_first.at[t], rows_second.at[t])
+        depth = width // 2
+        pieces[0][z] = normed[:, :depth]
+        pieces[1][z, :, :depth] = normed[:, depth:]
+        pieces[1][z, :, depth:] = sides[t].astype(jnp.bfloat16)
 
         @pl.when(t == 0)
         def _():
             pl.semaphore_wait(barrier, 5)
 
-        def share(src, dst, kind, peer):
+        def share(p, src, dst, kind, peer):
             return send(
-                rows.at[src], rows.at[dst], gather_send.at[t, kind, src], gather_recv.at[t, dst], peer
-            )
-
-        def landed(at):
-            arrived(rows.at[at], gather_send.at[t, 0, 0], gather_recv.at[t, at])
-
-        def to_next(at_z, up):
+                pieces[p].at[src], pieces[p].at[dst],
+                gather_send.at[t, p, kind, src], gather_recv.at[t, p, dst], peer,
+            )
+
+        def landed(p, at):
+            arrived(pieces[p].at[at], gather_send.at[t, p, 0, 0], gather_recv.at[t, p, at])
+
+        def to_next(p, at_z, up):
             @pl.when((z < CHIPS_Z - 1) if up else (z > 0))
             def _():
-                share(at_z, at_z, 0 if up else 1, device(z + 1 if up else z - 1, y, core))
-
-        to_next(z, True)
-        to_next(z, False)
-        share(z, CHIPS_Z + z, 2, across)
-        share(z, half + z, 3, sibling)
+                share(p, at_z, at_z, 0 if up else 1, device(z + 1 if up else z - 1, y, core))
+
+        for p in range(2):
+            to_next(p, z, True)
+            to_next(p, z, False)
+            share(p, z, CHIPS_Z + z, 2, across)
+            share(p, z, half + z, 3, sibling)
+
+        pl.when(t == 0)(count_pairs)
+
         for step in range(1, CHIPS_Z):
-            for up in (True, False):
-                at_z = z - step if up else z + step
-
-                @pl.when((at_z >= 0) if up else (at_z < CHIPS_Z))
-                def _(at_z=at_z, up=up):
-                    landed(at_z)
-                    to_next(at_z, up)
-                    share(at_z, CHIPS_Z + at_z, 2, across)
-                    share(at_z, half + at_z, 3, sibling)
+            for p in range(2):
+                for up in (True, False):
+                    at_z = z - step if up else z + step
+
+                    @pl.when((at_z >= 0) if up else (at_z < CHIPS_Z))
+                    def _(p=p, at_z=at_z, up=up):
+                        landed(p, at_z)
+                        to_next(p, at_z, up)
+                        share(p, at_z, CHIPS_Z + at_z, 2, across)
+                        share(p, at_z, half + at_z, 3, sibling)
+
+        def across_to_sibling(p, step):
+            ends = ((z, None),)
+            if step:
+                ends = ((z - step, z - step >= 0), (z + step, z + step < CHIPS_Z))
+            for at_z, there in ends:
+
+                def relay(at_z=at_z):
+                    landed(p, CHIPS_Z + at_z)
+                    share(p, CHIPS_Z + at_z, half + CHIPS_Z + at_z, 3, sibling)
+
+                if there is None:
+                    relay()
+                else:
+                    pl.when(there)(relay)
+
+        def piece(p):
+            return pieces[p][:, :, :depth].reshape(all_rows, depth)
+
+        def gate_up(p, at):
+            x = piece(p)
+            span = slice(p * depth, (p + 1) * depth)
+            return (
+                jnp.dot(x, w_gate[span, at], preferred_element_type=jnp.float32),
+                jnp.dot(x, w_up[span, at], preferred_element_type=jnp.float32),
+            )
+
+        for step in range(CHIPS_Z):
+            across_to_sibling(0, step)
+        for i in range(half):
+            landed(0, half + i)
 
         @pl.when(t == 0)
         def _():
             weights[0].wait()
             weights[1].wait()
 
-        def half_rows(dy, lanes):
-            pieces = [
-                rows[pl.ds(dc * half + dy * CHIPS_Z, CHIPS_Z), :, lanes] for dc in range(CORES)
-            ]
-            return jnp.concatenate(pieces, axis=0).reshape(all_rows // 2, -1)
-
-        def gate_up(dy):
-            span = slice(dy * all_rows // 2, (dy + 1) * all_rows // 2)
-
-            @pl.loop(0, hidden_width // TILE)
-            def _(i):
-                at = pl.ds(pl.multiple_of(i * TILE, TILE), TILE)
-                x = half_rows(dy, slice(0, width))
-                gate_val = jnp.dot(x, w_gate[:, at], preferred_element_type=jnp.float32)
-                up_val = jnp.dot(x, w_up[:, at], preferred_element_type=jnp.float32)
-                silu = gate_val / (1.0 + jnp.exp(-gate_val))
-                hidden[span, at] = (silu * up_val).astype(jnp.bfloat16)
-
-            side = half_rows(dy, slice(width, width + LANES)).astype(jnp.float32)
-            logits = lax.dot_general(
-                half_rows(dy, slice(0, width)), router[...],
+        for i in range(hidden_width // TILE):
+            at = slice(i * TILE, (i + 1) * TILE)
+            partial[0, :, at], partial[1, :, at] = gate_up(0, at)
+            if i < CHIPS_Z:
+                across_to_sibling(1, i)
+        for step in range(hidden_width // TILE, CHIPS_Z):
+            across_to_sibling(1, step)
+        for i in range(half):
+            landed(1, half + i)
+
+        @pl.loop(0, hidden_width // TILE)
+        def _(i):
+            at = pl.ds(pl.multiple_of(i * TILE, TILE), TILE)
+            gate_val, up_val = gate_up(1, at)
+            gate_val = partial[0, :, at] + gate_val
+            up_val = partial[1, :, at] + up_val
+            silu = gate_val / (1.0 + jnp.exp(-gate_val))
+            hidden[:, at] = (silu * up_val).astype(jnp.bfloat16)
+
+        side = pieces[1][:, :, depth:].reshape(all_rows, LANES).astype(jnp.float32)
+        logits = 0.0
+        for p in range(2):
+            logits += lax.dot_general(
+                piece(p), router[:, p * depth : (p + 1) * depth],
                 (((1,), (1,)), ((), ())), preferred_element_type=jnp.float32,
             )
-            sigma = side[:, :FUSED_DEVICES] / (1.0 + jnp.exp(-logits))
-            gates = sigma / jnp.sum(sigma, axis=1, keepdims=True)
-            gate_lane = lax.broadcasted_iota(jnp.int32, gates.shape, 1)
-            gate_col[span] = side[:, FLAG : FLAG + 1] * jnp.sum(
-                jnp.where(gate_lane == me, gates, 0.0), axis=1, keepdims=True
-            )
-
-        for i in range(CHIPS_Z):
-            landed(half + i)
-        for step in range(CHIPS_Z):
-            if step == 0:
-                landed(CHIPS_Z + z)
-                share(CHIPS_Z + z, half + CHIPS_Z + z, 3, sibling)
-                continue
-            for at_z, there in ((z - step, z - step >= 0), (z + step, z + step < CHIPS_Z)):
-
-                @pl.when(there)
-                def _(at_z=at_z):
-                    landed(CHIPS_Z + at_z)
-                    share(CHIPS_Z + at_z, half + CHIPS_Z + at_z, 3, sibling)
-
-            if step == 1:
-                gate_up(0)
-        for i in range(CHIPS_Z):
-            landed(half + CHIPS_Z + i)
-        gate_up(1)
+        sigma = side[:, :FUSED_DEVICES] / (1.0 + jnp.exp(-logits))
+        gates = sigma / jnp.sum(sigma, axis=1, keepdims=True)
+        gate_lane = lax.broadcasted_iota(jnp.int32, gates.shape, 1)
+        gate_col[...] = side[:, FLAG : FLAG + 1] * jnp.sum(
+            jnp.where(gate_lane == me, gates, 0.0), axis=1, keepdims=True
+        )
 
         @pl.when(t == iter_count - 1)
         def _():
-            total = jnp.sum(rows[:, :, width:].astype(jnp.float32), axis=0)
+            total = jnp.sum(pieces[1][:, :, depth:].astype(jnp.float32), axis=0)
             row_at = lax.broadcasted_iota(jnp.int32, total.shape, 0)
             own = jnp.sum(jnp.where(row_at == me, total, 0.0), axis=0, keepdims=True)
             load[...] = own[:, LOADS : LOADS + 2 * iter_count] / float(row_count * top_count)
@@ -281,10 +301,7 @@
             )
             outs = outs.astype(jnp.bfloat16).astype(jnp.float32) * gate_col[...]
             outs = outs.astype(jnp.bfloat16).reshape(FUSED_DEVICES, row_count, chunk)
-            for dy in range(CHIPS_Y):
-                for dc in range(CORES):
-                    first = (dy * CORES + dc) * CHIPS_Z
-                    part[t, c, pl.ds(dc * half + dy * CHIPS_Z, CHIPS_Z)] = outs[first : first + CHIPS_Z]
+            part[t, c] = outs
             sent.append(to_core(c))
             if c >= 2:
                 sent.append(to_y(c - 2))
@@ -297,19 +314,20 @@
         for copy in sent:
             copy.wait_send()
 
-        def gone(src, kind):
+        def gone(p, src, kind):
             pltpu.make_async_remote_copy(
-                src_ref=rows.at[src], dst_ref=rows.at[src],
-                send_sem=gather_send.at[t, kind, src], recv_sem=gather_recv.at[t, src],
+                src_ref=pieces[p].at[src], dst_ref=pieces[p].at[src],
+                send_sem=gather_send.at[t, p, kind, src], recv_sem=gather_recv.at[t, p, src],
                 device_id=sibling, device_id_type=pl.DeviceIdType.MESH,
             ).wait_send()
 
-        for at_z in range(CHIPS_Z):
-            pl.when((at_z <= z) & (z < CHIPS_Z - 1))(functools.partial(gone, at_z, 0))
-            pl.when((at_z >= z) & (z > 0))(functools.partial(gone, at_z, 1))
-            gone(at_z, 2)
-            gone(at_z, 3)
-            gone(CHIPS_Z + at_z, 3)
+        for p in range(2):
+            for at_z in range(CHIPS_Z):
+                pl.when((at_z <= z) & (z < CHIPS_Z - 1))(functools.partial(gone, p, at_z, 0))
+                pl.when((at_z >= z) & (z > 0))(functools.partial(gone, p, at_z, 1))
+                gone(p, at_z, 2)
+                gone(p, at_z, 3)
+                gone(p, CHIPS_Z + at_z, 3)
 
     out[...] = state[...].astype(jnp.bfloat16)
 
@@ -346,7 +364,10 @@
             pltpu.VMEM((hidden_width, width), bf16),
             pltpu.VMEM((row_count, width), f32),
             pltpu.VMEM((iter_count, row_count, LANES), f32),
-            pltpu.VMEM((iter_count, FUSED_DEVICES, row_count, width + LANES), bf16),
+            pltpu.VMEM((iter_count, row_count, LANES), f32),
+            pltpu.VMEM((iter_count, FUSED_DEVICES, row_count, width // 2), bf16),
+            pltpu.VMEM((iter_count, FUSED_DEVICES, row_count, width // 2 + LANES), bf16),
+            pltpu.VMEM((2, all_rows, hidden_width), f32),
             pltpu.VMEM((all_rows, hidden_width), bf16),
             pltpu.VMEM((all_rows, 1), f32),
             pltpu.VMEM((*per_chunk, FUSED_DEVICES, row_count, chunk), bf16),
@@ -357,8 +378,8 @@
             pltpu.VMEM((*per_chunk, CHIPS_Z - 1, row_count, chunk), bf16),
             dma((len(small),)),
             dma((3,)),
-            dma((iter_count, 4, FUSED_DEVICES)),
-            dma((iter_count, FUSED_DEVICES)),
+            dma((iter_count, 2, 4, FUSED_DEVICES)),
+            dma((iter_count, 2, FUSED_DEVICES)),
             dma(per_chunk),
             dma(per_chunk),
             dma(per_chunk),

time: 70.4 us -> 74 us (1.051)
  Pallas kernels: 67 us -> 70.6 us
    pallas_call x1, Pallas kernels: 67 us -> 70.6 us  [fused_body(): pl.pallas_call(fused_kernel, out_shape=(jax.ShapeDtypeStruct(tokens.shape...]
where the time goes in v3:
time: 74 us; the launch traced here: 73.8 us
  Pallas kernels  70.6 us (95%)
  local copies, waits for them, and re-layouts  2.59 us (4%)
    pallas_call x1, Pallas kernels, fused_body(): pl.pallas_call(fused_kernel, out_shape=(jax.ShapeDtypeStruct(tokens.shape...  70.6 us
    unnamed x2, local copies, waits for them, and re-layouts  2.59 us

profile of v3, /device:TPU:0, one launch (start us, length us, event | category | flops | bytes accessed | tf_op | source)
XLA Modules:
  0.0 73.8 jit_solution(10515562851840892009)
XLA Ops:
  0.6 70.6 %shard_map.113 = (bf16[16,2048]{1,0:T(8,128)(2,1)}, f32[1,4]{1,0:T(1,128)}) custom-call(bf16[16,2048]{1,0:T(8,128)(2,1)} %tokens_hbm.1, s32[1,16]{1,0:T(1,128)} %bitcast.6, s32[2,8,16]{2,1,0:T(8,128)} %bitcast.5, bf16[2048]{0:T(1024)(128)(2,1)} %gain_hbm.1, s32[1,16]{1,0:T(1,128)} %bitcast.7, s32[1,16]{1,0:T(1,128)} %choice_hbm.1, bf16[16,2048]{1,0:T(8,128)(2,1)} %bitcast.4, ...), custom_call_target="tpu_custom_call" | custom-call | flops 4831838208 | bytes 9437184 | tf_op jit(solution)/shard_map/pallas_call | solution.py:352
  71.2 1.5 %copy.14 = bf16[16,2048]{1,0:T(8,128)(2,1)} copy(bf16[16,2048]{1,0:T(8,128)(2,1)} %get-tuple-element.4) | data formatting | bytes 131072
  72.7 1.1 %copy.15 = f32[1,4]{1,0:T(1,128)} copy(f32[1,4]{1,0:T(1,128)} %get-tuple-element.5) | data formatting | bytes 32

commit v4 on v3

--- a/solution.py
+++ b/solution.py
@@ -1,5 +1,3 @@
-import functools
-
 import jax
 import jax.numpy as jnp
 from jax import lax
@@ -12,7 +10,7 @@
 LOADS = 48
 CORES, CHIPS_Y, CHIPS_Z = 2, 2, 4
 FUSED_DEVICES = CORES * CHIPS_Y * CHIPS_Z
-CHUNKS = 4
+CHUNKS = 2
 TILE = 256
 
 
@@ -21,7 +19,7 @@
     gate_hbm, up_hbm, down_hbm,
     out, load,
     tokens, depths, routes, gain, plan, choice, router, w_gate, w_up, w_down,
-    state, sides, masks, rows_first, rows_second, partial, hidden, gate_col,
+    state, sides, masks, rows_all, hidden, gate_col,
     part, from_core, for_y, from_y, for_z, from_z,
     small_sem, weight_sem, gather_send, gather_recv, core_send, core_recv, y_send, y_recv, z_send, z_recv,
 ):
@@ -128,112 +126,64 @@
         state32 = state[...]
         scale = lax.rsqrt(jnp.mean(state32 * state32, axis=1, keepdims=True) + 1e-06)
         normed = (state32 * scale * gain[...].reshape(1, width).astype(jnp.float32)).astype(jnp.bfloat16)
-        pieces = (rows_first.at[t], rows_second.at[t])
-        depth = width // 2
-        pieces[0][z] = normed[:, :depth]
-        pieces[1][z, :, :depth] = normed[:, depth:]
-        pieces[1][z, :, depth:] = sides[t].astype(jnp.bfloat16)
+        rows = rows_all.at[t]
+        rows[z, :, :width] = normed
+        rows[z, :, width:] = sides[t].astype(jnp.bfloat16)
 
         @pl.when(t == 0)
         def _():
             pl.semaphore_wait(barrier, 5)
 
-        def share(p, src, dst, kind, peer):
-            return send(
-                pieces[p].at[src], pieces[p].at[dst],
-                gather_send.at[t, p, kind, src], gather_recv.at[t, p, dst], peer,
+        sent = []
+
+        def share(src, dst, peer, blocks=1):
+            k = len(sent)
+            sent.append(
+                send(
+                    rows.at[pl.ds(src, blocks)], rows.at[pl.ds(dst, blocks)],
+                    gather_send.at[t, k], gather_recv.at[t, dst], peer,
+                )
             )
 
-        def landed(p, at):
-            arrived(pieces[p].at[at], gather_send.at[t, p, 0, 0], gather_recv.at[t, p, at])
-
-        def to_next(p, at_z, up):
-            @pl.when((z < CHIPS_Z - 1) if up else (z > 0))
-            def _():
-                share(p, at_z, at_z, 0 if up else 1, device(z + 1 if up else z - 1, y, core))
-
-        for p in range(2):
-            to_next(p, z, True)
-            to_next(p, z, False)
-            share(p, z, CHIPS_Z + z, 2, across)
-            share(p, z, half + z, 3, sibling)
-
+        def landed(at, blocks=1):
+            arrived(rows.at[pl.ds(at, blocks)], gather_send.at[t, 0], gather_recv.at[t, at])
+
+        share(z, CHIPS_Z + z, across)
+        for peer in along:
+            share(z, z, peer)
         pl.when(t == 0)(count_pairs)
-
-        for step in range(1, CHIPS_Z):
-            for p in range(2):
-                for up in (True, False):
-                    at_z = z - step if up else z + step
-
-                    @pl.when((at_z >= 0) if up else (at_z < CHIPS_Z))
-                    def _(p=p, at_z=at_z, up=up):
-                        landed(p, at_z)
-                        to_next(p, at_z, up)
-                        share(p, at_z, CHIPS_Z + at_z, 2, across)
-                        share(p, at_z, half + at_z, 3, sibling)
-
-        def across_to_sibling(p, step):
-            ends = ((z, None),)
-            if step:
-                ends = ((z - step, z - step >= 0), (z + step, z + step < CHIPS_Z))
-            for at_z, there in ends:
-
-                def relay(at_z=at_z):
-                    landed(p, CHIPS_Z + at_z)
-                    share(p, CHIPS_Z + at_z, half + CHIPS_Z + at_z, 3, sibling)
-
-                if there is None:
-                    relay()
-                else:
-                    pl.when(there)(relay)
-
-        def piece(p):
-            return pieces[p][:, :, :depth].reshape(all_rows, depth)
-
-        def gate_up(p, at):
-            x = piece(p)
-            span = slice(p * depth, (p + 1) * depth)
-            return (
-                jnp.dot(x, w_gate[span, at], preferred_element_type=jnp.float32),
-                jnp.dot(x, w_up[span, at], preferred_element_type=jnp.float32),
-            )
-
-        for step in range(CHIPS_Z):
-            across_to_sibling(0, step)
-        for i in range(half):
-            landed(0, half + i)
+        for at_z in other_z:
+            landed(at_z)
+            share(at_z, CHIPS_Z + at_z, across)
+        share(0, half, sibling, CHIPS_Z)
+        for at_z in (z, *other_z):
+            landed(CHIPS_Z + at_z)
+        share(CHIPS_Z, half + CHIPS_Z, sibling, CHIPS_Z)
 
         @pl.when(t == 0)
         def _():
             weights[0].wait()
             weights[1].wait()
 
-        for i in range(hidden_width // TILE):
-            at = slice(i * TILE, (i + 1) * TILE)
-            partial[0, :, at], partial[1, :, at] = gate_up(0, at)
-            if i < CHIPS_Z:
-                across_to_sibling(1, i)
-        for step in range(hidden_width // TILE, CHIPS_Z):
-            across_to_sibling(1, step)
-        for i in range(half):
-            landed(1, half + i)
+        for dy in range(CHIPS_Y):
+            landed(half + dy * CHIPS_Z, CHIPS_Z)
+
+        def flat_rows():
+            return rows[:, :, :width].reshape(all_rows, width)
 
         @pl.loop(0, hidden_width // TILE)
         def _(i):
             at = pl.ds(pl.multiple_of(i * TILE, TILE), TILE)
-            gate_val, up_val = gate_up(1, at)
-            gate_val = partial[0, :, at] + gate_val
-            up_val = partial[1, :, at] + up_val
+            x = flat_rows()
+            gate_val = jnp.dot(x, w_gate[:, at], preferred_element_type=jnp.float32)
+            up_val = jnp.dot(x, w_up[:, at], preferred_element_type=jnp.float32)
             silu = gate_val / (1.0 + jnp.exp(-gate_val))
             hidden[:, at] = (silu * up_val).astype(jnp.bfloat16)
 
-        side = pieces[1][:, :, depth:].reshape(all_rows, LANES).astype(jnp.float32)
-        logits = 0.0
-        for p in range(2):
-            logits += lax.dot_general(
-                piece(p), router[:, p * depth : (p + 1) * depth],
-                (((1,), (1,)), ((), ())), preferred_element_type=jnp.float32,
-            )
+        side = rows[:, :, width:].reshape(all_rows, LANES).astype(jnp.float32)
+        logits = lax.dot_general(
+            flat_rows(), router[...], (((1,), (1,)), ((), ())), preferred_element_type=jnp.float32
+        )
         sigma = side[:, :FUSED_DEVICES] / (1.0 + jnp.exp(-logits))
         gates = sigma / jnp.sum(sigma, axis=1, keepdims=True)
         gate_lane = lax.broadcasted_iota(jnp.int32, gates.shape, 1)
@@ -243,7 +193,7 @@
 
         @pl.when(t == iter_count - 1)
         def _():
-            total = jnp.sum(pieces[1][:, :, depth:].astype(jnp.float32), axis=0)
+            total = jnp.sum(rows[:, :, width:].astype(jnp.float32), axis=0)
             row_at = lax.broadcasted_iota(jnp.int32, total.shape, 0)
             own = jnp.sum(jnp.where(row_at == me, total, 0.0), axis=0, keepdims=True)
             load[...] = own[:, LOADS : LOADS + 2 * iter_count] / float(row_count * top_count)
@@ -293,7 +243,6 @@
             at = slice(c * chunk, (c + 1) * chunk)
             state[:, at] = (state[:, at] + total).astype(jnp.bfloat16).astype(jnp.float32)
 
-        sent = []
         for c in range(CHUNKS):
             outs = jnp.dot(
                 hidden[...], w_down[:, c * chunk : (c + 1) * chunk],
@@ -303,31 +252,15 @@
             outs = outs.astype(jnp.bfloat16).reshape(FUSED_DEVICES, row_count, chunk)
             part[t, c] = outs
             sent.append(to_core(c))
-            if c >= 2:
-                sent.append(to_y(c - 2))
-        for c in range(CHUNKS - 2, CHUNKS):
-            sent.append(to_y(c))
+            if c >= 1:
+                sent.append(to_y(c - 1))
+        sent.append(to_y(CHUNKS - 1))
         for c in range(CHUNKS):
             sent.extend(to_z(c))
         for c in range(CHUNKS):
             finish(c)
         for copy in sent:
             copy.wait_send()
-
-        def gone(p, src, kind):
-            pltpu.make_async_remote_copy(
-                src_ref=pieces[p].at[src], dst_ref=pieces[p].at[src],
-                send_sem=gather_send.at[t, p, kind, src], recv_sem=gather_recv.at[t, p, src],
-                device_id=sibling, device_id_type=pl.DeviceIdType.MESH,
-            ).wait_send()
-
-        for p in range(2):
-            for at_z in range(CHIPS_Z):
-                pl.when((at_z <= z) & (z < CHIPS_Z - 1))(functools.partial(gone, p, at_z, 0))
-                pl.when((at_z >= z) & (z > 0))(functools.partial(gone, p, at_z, 1))
-                gone(p, at_z, 2)
-                gone(p, at_z, 3)
-                gone(p, CHIPS_Z + at_z, 3)
 
     out[...] = state[...].astype(jnp.bfloat16)
 
@@ -365,9 +298,7 @@
             pltpu.VMEM((row_count, width), f32),
             pltpu.VMEM((iter_count, row_count, LANES), f32),
             pltpu.VMEM((iter_count, row_count, LANES), f32),
-            pltpu.VMEM((iter_count, FUSED_DEVICES, row_count, width // 2), bf16),
-            pltpu.VMEM((iter_count, FUSED_DEVICES, row_count, width // 2 + LANES), bf16),
-            pltpu.VMEM((2, all_rows, hidden_width), f32),
+            pltpu.VMEM((iter_count, FUSED_DEVICES, row_count, width + LANES), bf16),
             pltpu.VMEM((all_rows, hidden_width), bf16),
             pltpu.VMEM((all_rows, 1), f32),
             pltpu.VMEM((*per_chunk, FUSED_DEVICES, row_count, chunk), bf16),
@@ -378,8 +309,8 @@
             pltpu.VMEM((*per_chunk, CHIPS_Z - 1, row_count, chunk), bf16),
             dma((len(small),)),
             dma((3,)),
-            dma((iter_count, 2, 4, FUSED_DEVICES)),
-            dma((iter_count, 2, FUSED_DEVICES)),
+            dma((iter_count, FUSED_DEVICES)),
+            dma((iter_count, FUSED_DEVICES)),
             dma(per_chunk),
             dma(per_chunk),
             dma(per_chunk),

time: 74 us -> 68.4 us (0.924)
  Pallas kernels: 70.6 us -> 65 us
    pallas_call x1, Pallas kernels: 70.6 us -> 65 us  [fused_body(): pl.pallas_call(fused_kernel, out_shape=(jax.ShapeDtypeStruct(tokens.shape...]
where the time goes in v4:
time: 68.4 us; the launch traced here: 68.2 us
  Pallas kernels  65 us (95%)
  local copies, waits for them, and re-layouts  2.59 us (4%)
    pallas_call x1, Pallas kernels, fused_body(): pl.pallas_call(fused_kernel, out_shape=(jax.ShapeDtypeStruct(tokens.shape...  65 us
    unnamed x2, local copies, waits for them, and re-layouts  2.59 us

profile of v4, /device:TPU:0, one launch (start us, length us, event | category | flops | bytes accessed | tf_op | source)
XLA Modules:
  0.0 68.2 jit_solution(17249218058114853898)
XLA Ops:
  0.6 65.0 %shard_map.113 = (bf16[16,2048]{1,0:T(8,128)(2,1)}, f32[1,4]{1,0:T(1,128)}) custom-call(bf16[16,2048]{1,0:T(8,128)(2,1)} %tokens_hbm.1, s32[1,16]{1,0:T(1,128)} %bitcast.6, s32[2,8,16]{2,1,0:T(8,128)} %bitcast.5, bf16[2048]{0:T(1024)(128)(2,1)} %gain_hbm.1, s32[1,16]{1,0:T(1,128)} %bitcast.7, s32[1,16]{1,0:T(1,128)} %choice_hbm.1, bf16[16,2048]{1,0:T(8,128)(2,1)} %bitcast.4, ...), custom_call_target="tpu_custom_call" | custom-call | flops 4831838208 | bytes 9437184 | tf_op jit(solution)/shard_map/pallas_call | solution.py:285
  65.6 1.5 %copy.14 = bf16[16,2048]{1,0:T(8,128)(2,1)} copy(bf16[16,2048]{1,0:T(8,128)(2,1)} %get-tuple-element.4) | data formatting | bytes 131072
  67.1 1.1 %copy.15 = f32[1,4]{1,0:T(1,128)} copy(f32[1,4]{1,0:T(1,128)} %get-tuple-element.5) | data formatting | bytes 32

commit v5 on v4

--- a/solution.py
+++ b/solution.py
@@ -10,7 +10,7 @@
 LOADS = 48
 CORES, CHIPS_Y, CHIPS_Z = 2, 2, 4
 FUSED_DEVICES = CORES * CHIPS_Y * CHIPS_Z
-CHUNKS = 2
+CHUNKS = 4
 TILE = 256
 
 

time: 68.4 us -> 65.7 us (0.961)
  Pallas kernels: 65 us -> 62.3 us
    pallas_call x1, Pallas kernels: 65 us -> 62.3 us  [fused_body(): pl.pallas_call(fused_kernel, out_shape=(jax.ShapeDtypeStruct(tokens.shape...]
where the time goes in v5:
time: 65.7 us; the launch traced here: 65.5 us
  Pallas kernels  62.3 us (95%)
  local copies, waits for them, and re-layouts  2.59 us (4%)
    pallas_call x1, Pallas kernels, fused_body(): pl.pallas_call(fused_kernel, out_shape=(jax.ShapeDtypeStruct(tokens.shape...  62.3 us
    unnamed x2, local copies, waits for them, and re-layouts  2.59 us

profile of v5, /device:TPU:0, one launch (start us, length us, event | category | flops | bytes accessed | tf_op | source)
XLA Modules:
  0.0 65.5 jit_solution(8370860719924601095)
XLA Ops:
  0.6 62.3 %shard_map.113 = (bf16[16,2048]{1,0:T(8,128)(2,1)}, f32[1,4]{1,0:T(1,128)}) custom-call(bf16[16,2048]{1,0:T(8,128)(2,1)} %tokens_hbm.1, s32[1,16]{1,0:T(1,128)} %bitcast.6, s32[2,8,16]{2,1,0:T(8,128)} %bitcast.5, bf16[2048]{0:T(1024)(128)(2,1)} %gain_hbm.1, s32[1,16]{1,0:T(1,128)} %bitcast.7, s32[1,16]{1,0:T(1,128)} %choice_hbm.1, bf16[16,2048]{1,0:T(8,128)(2,1)} %bitcast.4, ...), custom_call_target="tpu_custom_call" | custom-call | flops 4831838208 | bytes 9437184 | tf_op jit(solution)/shard_map/pallas_call | solution.py:285
  62.9 1.5 %copy.14 = bf16[16,2048]{1,0:T(8,128)(2,1)} copy(bf16[16,2048]{1,0:T(8,128)(2,1)} %get-tuple-element.4) | data formatting | bytes 131072
  64.4 1.1 %copy.15 = f32[1,4]{1,0:T(1,128)} copy(f32[1,4]{1,0:T(1,128)} %get-tuple-element.5) | data formatting | bytes 32

commit v6 on v5

--- a/solution.py
+++ b/solution.py
@@ -10,7 +10,7 @@
 LOADS = 48
 CORES, CHIPS_Y, CHIPS_Z = 2, 2, 4
 FUSED_DEVICES = CORES * CHIPS_Y * CHIPS_Z
-CHUNKS = 4
+CHUNKS = 8
 TILE = 256
 
 

time: 65.7 us -> 69.4 us (1.056)
  Pallas kernels: 62.3 us -> 66 us
    pallas_call x1, Pallas kernels: 62.3 us -> 66 us  [fused_body(): pl.pallas_call(fused_kernel, out_shape=(jax.ShapeDtypeStruct(tokens.shape...]
where the time goes in v6:
time: 69.4 us; the launch traced here: 69.2 us
  Pallas kernels  66 us (95%)
  local copies, waits for them, and re-layouts  2.59 us (4%)
    pallas_call x1, Pallas kernels, fused_body(): pl.pallas_call(fused_kernel, out_shape=(jax.ShapeDtypeStruct(tokens.shape...  66 us
    unnamed x2, local copies, waits for them, and re-layouts  2.59 us

profile of v6, /device:TPU:0, one launch (start us, length us, event | category | flops | bytes accessed | tf_op | source)
XLA Modules:
  0.0 69.2 jit_solution(12807887964806644515)
XLA Ops:
  0.6 66.0 %shard_map.113 = (bf16[16,2048]{1,0:T(8,128)(2,1)}, f32[1,4]{1,0:T(1,128)}) custom-call(bf16[16,2048]{1,0:T(8,128)(2,1)} %tokens_hbm.1, s32[1,16]{1,0:T(1,128)} %bitcast.6, s32[2,8,16]{2,1,0:T(8,128)} %bitcast.5, bf16[2048]{0:T(1024)(128)(2,1)} %gain_hbm.1, s32[1,16]{1,0:T(1,128)} %bitcast.7, s32[1,16]{1,0:T(1,128)} %choice_hbm.1, bf16[16,2048]{1,0:T(8,128)(2,1)} %bitcast.4, ...), custom_call_target="tpu_custom_call" | custom-call | flops 4831838208 | bytes 9437184 | tf_op jit(solution)/shard_map/pallas_call | solution.py:285
  66.6 1.5 %copy.14 = bf16[16,2048]{1,0:T(8,128)(2,1)} copy(bf16[16,2048]{1,0:T(8,128)(2,1)} %get-tuple-element.4) | data formatting | bytes 131072
  68.1 1.1 %copy.15 = f32[1,4]{1,0:T(1,128)} copy(f32[1,4]{1,0:T(1,128)} %get-tuple-element.5) | data formatting | bytes 32

commit v7 on v5

--- a/solution.py
+++ b/solution.py
@@ -160,6 +160,23 @@
             landed(CHIPS_Z + at_z)
         share(CHIPS_Z, half + CHIPS_Z, sibling, CHIPS_Z)
 
+        def gates_of(first):
+            here = rows[first : first + half]
+            side = here[:, :, width:].reshape(all_rows // 2, LANES).astype(jnp.float32)
+            logits = lax.dot_general(
+                here[:, :, :width].reshape(all_rows // 2, width), router[...],
+                (((1,), (1,)), ((), ())), preferred_element_type=jnp.float32,
+            )
+            sigma = side[:, :FUSED_DEVICES] / (1.0 + jnp.exp(-logits))
+            gates = sigma / jnp.sum(sigma, axis=1, keepdims=True)
+            gate_lane = lax.broadcasted_iota(jnp.int32, gates.shape, 1)
+            span = slice(first * row_count, (first + half) * row_count)
+            gate_col[span] = side[:, FLAG : FLAG + 1] * jnp.sum(
+                jnp.where(gate_lane == me, gates, 0.0), axis=1, keepdims=True
+            )
+
+        gates_of(0)
+
         @pl.when(t == 0)
         def _():
             weights[0].wait()
@@ -180,23 +197,7 @@
             silu = gate_val / (1.0 + jnp.exp(-gate_val))
             hidden[:, at] = (silu * up_val).astype(jnp.bfloat16)
 
-        side = rows[:, :, width:].reshape(all_rows, LANES).astype(jnp.float32)
-        logits = lax.dot_general(
-            flat_rows(), router[...], (((1,), (1,)), ((), ())), preferred_element_type=jnp.float32
-        )
-        sigma = side[:, :FUSED_DEVICES] / (1.0 + jnp.exp(-logits))
-        gates = sigma / jnp.sum(sigma, axis=1, keepdims=True)
-        gate_lane = lax.broadcasted_iota(jnp.int32, gates.shape, 1)
-        gate_col[...] = side[:, FLAG : FLAG + 1] * jnp.sum(
-            jnp.where(gate_lane == me, gates, 0.0), axis=1, keepdims=True
-        )
-
-        @pl.when(t == iter_count - 1)
-        def _():
-            total = jnp.sum(rows[:, :, width:].astype(jnp.float32), axis=0)
-            row_at = lax.broadcasted_iota(jnp.int32, total.shape, 0)
-            own = jnp.sum(jnp.where(row_at == me, total, 0.0), axis=0, keepdims=True)
-            load[...] = own[:, LOADS : LOADS + 2 * iter_count] / float(row_count * top_count)
+        gates_of(half)
 
         @pl.when(t == 0)
         def _():
@@ -255,6 +256,14 @@
             if c >= 1:
                 sent.append(to_y(c - 1))
         sent.append(to_y(CHUNKS - 1))
+
+        @pl.when(t == iter_count - 1)
+        def _():
+            total = jnp.sum(rows[:, :, width:].astype(jnp.float32), axis=0)
+            row_at = lax.broadcasted_iota(jnp.int32, total.shape, 0)
+            own = jnp.sum(jnp.where(row_at == me, total, 0.0), axis=0, keepdims=True)
+            load[...] = own[:, LOADS : LOADS + 2 * iter_count] / float(row_count * top_count)
+
         for c in range(CHUNKS):
             sent.extend(to_z(c))
         for c in range(CHUNKS):

time: 65.7 us -> 65.1 us (level)
  no operation moved by 1% of the time
where the time goes in v7:
time: 65.1 us; the launch traced here: 64.9 us
  Pallas kernels  61.7 us (95%)
  local copies, waits for them, and re-layouts  2.59 us (4%)
    pallas_call x1, Pallas kernels, fused_body(): pl.pallas_call(fused_kernel, out_shape=(jax.ShapeDtypeStruct(tokens.shape...  61.7 us
    unnamed x2, local copies, waits for them, and re-layouts  2.59 us

profile of v7, /device:TPU:0, one launch (start us, length us, event | category | flops | bytes accessed | tf_op | source)
XLA Modules:
  0.0 64.9 jit_solution(6260647962281332050)
XLA Ops:
  0.6 61.7 %shard_map.113 = (bf16[16,2048]{1,0:T(8,128)(2,1)}, f32[1,4]{1,0:T(1,128)}) custom-call(bf16[16,2048]{1,0:T(8,128)(2,1)} %tokens_hbm.1, s32[1,16]{1,0:T(1,128)} %bitcast.6, s32[2,8,16]{2,1,0:T(8,128)} %bitcast.5, bf16[2048]{0:T(1024)(128)(2,1)} %gain_hbm.1, s32[1,16]{1,0:T(1,128)} %bitcast.7, s32[1,16]{1,0:T(1,128)} %choice_hbm.1, bf16[16,2048]{1,0:T(8,128)(2,1)} %bitcast.4, ...), custom_call_target="tpu_custom_call" | custom-call | flops 4831838208 | bytes 9437184 | tf_op jit(solution)/shard_map/pallas_call | solution.py:294
  62.3 1.5 %copy.14 = bf16[16,2048]{1,0:T(8,128)(2,1)} copy(bf16[16,2048]{1,0:T(8,128)(2,1)} %get-tuple-element.4) | data formatting | bytes 131072
  63.8 1.1 %copy.15 = f32[1,4]{1,0:T(1,128)} copy(f32[1,4]{1,0:T(1,128)} %get-tuple-element.5) | data formatting | bytes 32
